TPU v7x, 32 devices: a whole 2x2x4 slice. The times are simulated.
32 devices in a mesh: seq: 4 (over y, x), fsdp: 8 (over z, core).
Axes of the slice: x: 2, y: 2, z: 4, core: 2. Of those that a mesh axis runs over, the one named last changes fastest.
Arguments:
- tokens: bfloat16 [16, 2048, 768], P('fsdp', 'seq'), may hold values from -6 to 6
- segments: int32 [16, 2048], P('fsdp', 'seq'), may hold values from 0 to 31, never falling along the last dimension, each value on 1 to 1024 neighbouring positions
- qkv_weight: bfloat16 [768, 2304], P(('seq', 'fsdp')), may hold values from -0.21875 to 0.21875
- query_bias: bfloat16 [768], P(('seq', 'fsdp')), may hold values from -3 to 3
- value_bias: bfloat16 [768], P(('seq', 'fsdp')), may hold values from -3 to 3
- proj_weight: bfloat16 [768, 768], P(('seq', 'fsdp')), may hold values from -0.875 to 0.875
- proj_bias: bfloat16 [768], P(('seq', 'fsdp')), may hold values from -2 to 2
- attn_gain: bfloat16 [768], P(('seq', 'fsdp')), may hold values from 0.5 to 1.5
- attn_shift: bfloat16 [768], P(('seq', 'fsdp')), may hold values from -2 to 2
- ffn_gain: bfloat16 [768], P(('seq', 'fsdp')), may hold values from 0.5 to 1.5
- ffn_shift: bfloat16 [768], P(('seq', 'fsdp')), may hold values from -2 to 2
- expand_weight: bfloat16 [768, 3072], P(('seq', 'fsdp')), may hold values from -0.21875 to 0.21875
- expand_bias: bfloat16 [3072], P(('seq', 'fsdp')), may hold values from -3 to 3
- contract_weight: bfloat16 [3072, 768], P(('seq', 'fsdp')), may hold values from -0.109375 to 0.109375
- contract_bias: bfloat16 [768], P(('seq', 'fsdp')), may hold values from -2 to 2
- cotangent: bfloat16 [16, 2048, 768], P('fsdp', 'seq'), may hold values from -6 to 6
Outputs:
- outputs: bfloat16 [16, 2048, 768], P('fsdp', 'seq')
- token_grad: bfloat16 [16, 2048, 768], P('fsdp', 'seq')
- qkv_weight_grad: float32 [768, 2304], P(('seq', 'fsdp'))
- query_bias_grad: float32 [768], P(('seq', 'fsdp'))
- value_bias_grad: float32 [768], P(('seq', 'fsdp'))
- proj_weight_grad: float32 [768, 768], P(('seq', 'fsdp'))
- proj_bias_grad: float32 [768], P(('seq', 'fsdp'))
- attn_gain_grad: float32 [768], P(('seq', 'fsdp'))
- attn_shift_grad: float32 [768], P(('seq', 'fsdp'))
- ffn_gain_grad: float32 [768], P(('seq', 'fsdp'))
- ffn_shift_grad: float32 [768], P(('seq', 'fsdp'))
- expand_weight_grad: float32 [768, 3072], P(('seq', 'fsdp'))
- expand_bias_grad: float32 [3072], P(('seq', 'fsdp'))
- contract_weight_grad: float32 [3072, 768], P(('seq', 'fsdp'))
- contract_bias_grad: float32 [768], P(('seq', 'fsdp'))
Inputs may be any that keep to these rules, and one draw needn't show every extreme that they name: `segments`: within each packed sequence the document number never falls; every document holds 1 to 1024 tokens and one holds exactly 1024.
All inputs are finite; a program needn't handle non-finite values.
Results may differ from a plain program's by a relative error of at most 0.011.
Values may be sent and summed in bfloat16 or wider, within the bound.
No kernel may reach another device: no remote copies, remote signals or barrier semaphores. Data moves between devices by JAX's collectives and lax.ppermute only.
A program may use at most 192 MiB of HBM per device.

v0:
```python
import math

import jax
import jax.numpy as jnp
from jax import lax
from jax.sharding import PartitionSpec as P

HEADS = 12
HD = 64


NORM_EPS = 1e-05
MASKED_SCORE = -1e30


def norm_rows(values_in, norm_gain, norm_shift):
    row_mean = jnp.mean(values_in, axis=-1, keepdims=True)
    centered = values_in - row_mean
    row_var = jnp.mean(centered * centered, axis=-1, keepdims=True)
    return centered * lax.rsqrt(row_var + NORM_EPS) * norm_gain + norm_shift


def gelu_tanh(values_in):
    return (
        0.5
        * values_in
        * (
            1.0
            + jnp.tanh(
                0.7978845608028654 * (values_in + 0.044715 * values_in * values_in * values_in)
            )
        )
    )


def body(
    tokens,
    segments,
    qkv_weight,
    query_bias,
    value_bias,
    proj_weight,
    proj_bias,
    attn_gain,
    attn_shift,
    ffn_gain,
    ffn_shift,
    expand_weight,
    expand_bias,
    contract_weight,
    contract_bias,
    cotangent,
):
    gathered = (
        lax.all_gather(qkv_weight, ("seq", "fsdp"), axis=0, tiled=True),
        lax.all_gather(query_bias, ("seq", "fsdp"), axis=0, tiled=True),
        lax.all_gather(value_bias, ("seq", "fsdp"), axis=0, tiled=True),
        lax.all_gather(proj_weight, ("seq", "fsdp"), axis=0, tiled=True),
        lax.all_gather(proj_bias, ("seq", "fsdp"), axis=0, tiled=True),
        lax.all_gather(attn_gain, ("seq", "fsdp"), axis=0, tiled=True),
        lax.all_gather(attn_shift, ("seq", "fsdp"), axis=0, tiled=True),
        lax.all_gather(ffn_gain, ("seq", "fsdp"), axis=0, tiled=True),
        lax.all_gather(ffn_shift, ("seq", "fsdp"), axis=0, tiled=True),
        lax.all_gather(expand_weight, ("seq", "fsdp"), axis=0, tiled=True),
        lax.all_gather(expand_bias, ("seq", "fsdp"), axis=0, tiled=True),
        lax.all_gather(contract_weight, ("seq", "fsdp"), axis=0, tiled=True),
        lax.all_gather(contract_bias, ("seq", "fsdp"), axis=0, tiled=True),
    )
    (
        qkv_matrix,
        query_offset,
        value_offset,
        proj_matrix,
        proj_offset,
        attn_scale,
        attn_offset,
        ffn_scale,
        ffn_offset,
        expand_matrix,
        expand_offset,
        contract_matrix,
        contract_offset,
    ) = gathered
    micro_count, local_len, width = tokens.shape
    seq_parts = lax.axis_size("seq")
    heads_here = HEADS // seq_parts
    part_width = width // seq_parts
    token_count = micro_count * local_len
    whole_segments = lax.all_gather(segments, "seq", axis=1, tiled=True)
    seq_len = whole_segments.shape[1]
    block_len = min(512, seq_len)
    block_count = seq_len // block_len
    score_scale = 1.0 / math.sqrt(HD)
    positions = jnp.arange(seq_len, dtype=jnp.int32)
    token_rows = tokens.reshape(token_count, width).astype(jnp.float32)
    normed_one, pull_attn_norm = jax.vjp(
        norm_rows, token_rows, attn_scale.astype(jnp.float32), attn_offset.astype(jnp.float32)
    )
    normed_one = normed_one.astype(jnp.bfloat16)
    mixed_rows = jnp.dot(normed_one, qkv_matrix, preferred_element_type=jnp.float32)
    query_rows = mixed_rows[:, :width] + query_offset.astype(jnp.float32)
    key_rows = mixed_rows[:, width : 2 * width]
    value_rows = mixed_rows[:, 2 * width :] + value_offset.astype(jnp.float32)
    packed = (
        jnp.stack([query_rows, key_rows, value_rows])
        .astype(jnp.bfloat16)
        .reshape(3, micro_count, local_len, width)
    )
    by_heads = lax.all_to_all(packed, "seq", split_axis=3, concat_axis=2, tiled=True)
    split_heads = by_heads.reshape(3, micro_count, seq_len, heads_here, HD)
    query_heads = split_heads[0]
    key_heads = split_heads[1]
    value_heads = split_heads[2]

    def block_scores(micro_idx, block_start):
        query_all = lax.dynamic_index_in_dim(query_heads, micro_idx, 0, keepdims=False)
        query_block = lax.dynamic_slice_in_dim(query_all, block_start, block_len, 0)
        key_all = lax.dynamic_index_in_dim(key_heads, micro_idx, 0, keepdims=False)
        seg_all = lax.dynamic_index_in_dim(whole_segments, micro_idx, 0, keepdims=False)
        seg_block = lax.dynamic_slice_in_dim(seg_all, block_start, block_len, 0)
        query_pos = block_start + jnp.arange(block_len, dtype=jnp.int32)
        allowed = (query_pos[:, None] >= positions[None, :]) & (
            seg_block[:, None] == seg_all[None, :]
        )
        raw_scores = (
            jnp.einsum("qhd,khd->hqk", query_block, key_all, preferred_element_type=jnp.float32)
            * score_scale
        )
        return (query_block, key_all, jnp.where(allowed[None], raw_scores, MASKED_SCORE))

    def forward_block(block_index):
        micro_idx = block_index // block_count
        block_start = block_index % block_count * block_len
        query_block, key_all, scores = block_scores(micro_idx, block_start)
        value_all = lax.dynamic_index_in_dim(value_heads, micro_idx, 0, keepdims=False)
        row_max = jnp.max(scores, axis=-1, keepdims=True)
        shifted = jnp.exp(scores - row_max)
        row_total = jnp.sum(shifted, axis=-1, keepdims=True)
        soft_probs = (shifted / row_total).astype(jnp.bfloat16)
        block_out = jnp.einsum(
            "hqk,khd->qhd", soft_probs, value_all, preferred_element_type=jnp.float32
        ).astype(jnp.bfloat16)
        return (block_out, (row_max + jnp.log(row_total))[..., 0])

    block_outs, log_totals = lax.map(
        forward_block, jnp.arange(micro_count * block_count, dtype=jnp.int32)
    )
    attended_heads = block_outs.reshape(micro_count, seq_len, part_width)
    attended = lax.all_to_all(attended_heads, "seq", split_axis=1, concat_axis=2, tiled=True)
    attended_rows = attended.reshape(token_count, width)
    branch = jnp.dot(
        attended_rows, proj_matrix, preferred_element_type=jnp.float32
    ) + proj_offset.astype(jnp.float32)
    middle = token_rows + branch
    normed_two, pull_ffn_norm = jax.vjp(
        norm_rows, middle, ffn_scale.astype(jnp.float32), ffn_offset.astype(jnp.float32)
    )
    normed_two = normed_two.astype(jnp.bfloat16)
    hidden = jnp.dot(
        normed_two, expand_matrix, preferred_element_type=jnp.float32
    ) + expand_offset.astype(jnp.float32)
    active, pull_gelu = jax.vjp(gelu_tanh, hidden)
    active = active.astype(jnp.bfloat16)
    output_rows = jnp.dot(
        active, contract_matrix, preferred_element_type=jnp.float32
    ) + contract_offset.astype(jnp.float32)
    result = (middle + output_rows).astype(jnp.bfloat16).reshape(tokens.shape)
    qkv_back, proj_back, expand_back, contract_back = (
        lax.all_gather(qkv_weight, ("seq", "fsdp"), axis=0, tiled=True),
        lax.all_gather(proj_weight, ("seq", "fsdp"), axis=0, tiled=True),
        lax.all_gather(expand_weight, ("seq", "fsdp"), axis=0, tiled=True),
        lax.all_gather(contract_weight, ("seq", "fsdp"), axis=0, tiled=True),
    )
    out_grad = cotangent.reshape(token_count, width)
    contract_offset_grad = jnp.sum(out_grad.astype(jnp.float32), axis=0)
    contract_matrix_grad = jnp.einsum(
        "nf,nd->fd", active, out_grad, preferred_element_type=jnp.float32
    )
    active_grad = jnp.einsum(
        "nd,fd->nf", out_grad, contract_back, preferred_element_type=jnp.float32
    )
    hidden_grad = pull_gelu(active_grad)[0].astype(jnp.bfloat16)
    expand_offset_grad = jnp.sum(hidden_grad.astype(jnp.float32), axis=0)
    expand_matrix_grad = jnp.einsum(
        "nd,nf->df", normed_two, hidden_grad, preferred_element_type=jnp.float32
    )
    normed_two_grad = jnp.einsum(
        "nf,df->nd", hidden_grad, expand_back, preferred_element_type=jnp.float32
    )
    middle_part, ffn_scale_grad, ffn_offset_grad = pull_ffn_norm(normed_two_grad)
    middle_grad = out_grad.astype(jnp.float32) + middle_part
    branch_grad = middle_grad.astype(jnp.bfloat16)
    proj_offset_grad = jnp.sum(branch_grad.astype(jnp.float32), axis=0)
    proj_matrix_grad = jnp.einsum(
        "nd,ne->de", attended_rows, branch_grad, preferred_element_type=jnp.float32
    )
    attended_grad = jnp.einsum(
        "ne,de->nd", branch_grad, proj_back, preferred_element_type=jnp.float32
    )
    attended_grad = attended_grad.astype(jnp.bfloat16).reshape(micro_count, local_len, width)
    grad_heads = lax.all_to_all(attended_grad, "seq", split_axis=2, concat_axis=1, tiled=True)
    grad_heads = grad_heads.reshape(micro_count, seq_len, heads_here, HD)

    def backward_micro(micro_idx):
        value_all = lax.dynamic_index_in_dim(value_heads, micro_idx, 0, keepdims=False)
        grad_all = lax.dynamic_index_in_dim(grad_heads, micro_idx, 0, keepdims=False)

        def back_step(carry_pair, block_idx):
            key_acc, value_acc = carry_pair
            block_start = block_idx * block_len
            query_block, key_all, scores = block_scores(micro_idx, block_start)
            log_block = lax.dynamic_index_in_dim(
                log_totals, micro_idx * block_count + block_idx, 0, keepdims=False
            )
            soft_probs = jnp.exp(scores - log_block[..., None])
            probs_low = soft_probs.astype(jnp.bfloat16)
            grad_block = lax.dynamic_slice_in_dim(grad_all, block_start, block_len, 0)
            probs_grad = jnp.einsum(
                "qhd,khd->hqk", grad_block, value_all, preferred_element_type=jnp.float32
            )
            value_acc = value_acc + jnp.einsum(
                "hqk,qhd->khd", probs_low, grad_block, preferred_element_type=jnp.float32
            )
            score_grad = soft_probs * (
                probs_grad - jnp.sum(soft_probs * probs_grad, axis=-1, keepdims=True)
            )
            score_low = score_grad.astype(jnp.bfloat16)
            query_part = (
                jnp.einsum("hqk,khd->qhd", score_low, key_all, preferred_element_type=jnp.float32)
                * score_scale
            )
            key_acc = (
                key_acc
                + jnp.einsum(
                    "hqk,qhd->khd", score_low, query_block, preferred_element_type=jnp.float32
                )
                * score_scale
            )
            return ((key_acc, value_acc), query_part)

        empty_acc = jnp.zeros((seq_len, heads_here, HD), jnp.float32)
        (key_sum, value_sum), query_parts = lax.scan(
            back_step, (empty_acc, empty_acc), jnp.arange(block_count, dtype=jnp.int32)
        )
        return (query_parts.reshape(seq_len, heads_here, HD), key_sum, value_sum)

    query_grad, key_grad, value_grad = lax.map(
        backward_micro, jnp.arange(micro_count, dtype=jnp.int32)
    )
    grad_packed = (
        jnp.stack([query_grad, key_grad, value_grad])
        .astype(jnp.bfloat16)
        .reshape(3, micro_count, seq_len, part_width)
    )
    grad_tokens = lax.all_to_all(grad_packed, "seq", split_axis=2, concat_axis=3, tiled=True)
    grad_tokens = grad_tokens.reshape(3, token_count, width)
    query_offset_grad = jnp.sum(grad_tokens[0].astype(jnp.float32), axis=0)
    value_offset_grad = jnp.sum(grad_tokens[2].astype(jnp.float32), axis=0)
    qkv_matrix_grad = jnp.einsum(
        "nd,snf->dsf", normed_one, grad_tokens, preferred_element_type=jnp.float32
    ).reshape(width, 3 * width)
    normed_one_grad = jnp.einsum(
        "snf,dsf->nd",
        grad_tokens,
        qkv_back.reshape(width, 3, width),
        preferred_element_type=jnp.float32,
    )
    token_part, attn_scale_grad, attn_offset_grad = pull_attn_norm(normed_one_grad)
    token_grad = (middle_grad + token_part).astype(jnp.bfloat16).reshape(tokens.shape)
    summed = (
        lax.psum_scatter(qkv_matrix_grad, ("seq", "fsdp"), scatter_dimension=0, tiled=True),
        lax.psum_scatter(query_offset_grad, ("seq", "fsdp"), scatter_dimension=0, tiled=True),
        lax.psum_scatter(value_offset_grad, ("seq", "fsdp"), scatter_dimension=0, tiled=True),
        lax.psum_scatter(proj_matrix_grad, ("seq", "fsdp"), scatter_dimension=0, tiled=True),
        lax.psum_scatter(proj_offset_grad, ("seq", "fsdp"), scatter_dimension=0, tiled=True),
        lax.psum_scatter(attn_scale_grad, ("seq", "fsdp"), scatter_dimension=0, tiled=True),
        lax.psum_scatter(attn_offset_grad, ("seq", "fsdp"), scatter_dimension=0, tiled=True),
        lax.psum_scatter(ffn_scale_grad, ("seq", "fsdp"), scatter_dimension=0, tiled=True),
        lax.psum_scatter(ffn_offset_grad, ("seq", "fsdp"), scatter_dimension=0, tiled=True),
        lax.psum_scatter(expand_matrix_grad, ("seq", "fsdp"), scatter_dimension=0, tiled=True),
        lax.psum_scatter(expand_offset_grad, ("seq", "fsdp"), scatter_dimension=0, tiled=True),
        lax.psum_scatter(contract_matrix_grad, ("seq", "fsdp"), scatter_dimension=0, tiled=True),
        lax.psum_scatter(contract_offset_grad, ("seq", "fsdp"), scatter_dimension=0, tiled=True),
    )
    return (
        result,
        token_grad,
        summed[0],
        summed[1],
        summed[2],
        summed[3],
        summed[4],
        summed[5],
        summed[6],
        summed[7],
        summed[8],
        summed[9],
        summed[10],
        summed[11],
        summed[12],
    )


def solution(mesh):
    placed = (
        P("fsdp", "seq", None),
        P("fsdp", "seq"),
        P(("seq", "fsdp"), None),
        P(("seq", "fsdp")),
        P(("seq", "fsdp")),
        P(("seq", "fsdp"), None),
        P(("seq", "fsdp")),
        P(("seq", "fsdp")),
        P(("seq", "fsdp")),
        P(("seq", "fsdp")),
        P(("seq", "fsdp")),
        P(("seq", "fsdp"), None),
        P(("seq", "fsdp")),
        P(("seq", "fsdp"), None),
        P(("seq", "fsdp")),
        P("fsdp", "seq", None),
    )
    return jax.shard_map(
        body,
        mesh=mesh,
        in_specs=placed,
        out_specs=(
            P("fsdp", "seq", None),
            P("fsdp", "seq", None),
            P(("seq", "fsdp"), None),
            P(("seq", "fsdp")),
            P(("seq", "fsdp")),
            P(("seq", "fsdp"), None),
            P(("seq", "fsdp")),
            P(("seq", "fsdp")),
            P(("seq", "fsdp")),
            P(("seq", "fsdp")),
            P(("seq", "fsdp")),
            P(("seq", "fsdp"), None),
            P(("seq", "fsdp")),
            P(("seq", "fsdp"), None),
            P(("seq", "fsdp")),
        ),
        check_vma=False,
    )
```

profile of v0, /device:TPU:0, one launch (start us, length us, event | category | flops | bytes accessed | tf_op | source)
XLA Modules:
  0.0 1113.4 jit_solution(13760745855562202753)
XLA Ops:
  16.0 42.7 %all-reduce.19 = (bf16[768]{0:T(1024)(128)(2,1)S(1)}, bf16[768]{0:T(1024)(128)(2,1)S(1)}, bf16[768]{0:T(1024)(128)(2,1)S(1)}, bf16[768]{0:T(1024)(128)(2,1)S(1)}...) all-reduce(bf16[768]{0:T(1024)(128)(2,1)S(1)} %dynamic-update-slice, ...), channel_id=1, replica_groups=mesh['seq'=4,'fsdp'=8] {'seq','fsdp'}, use_global_device_ids=true, to_apply=%add.1 | all-reduce | flops 9216 | bytes 36864
  60.0 14.2 %all-gather.5.cloned.1.call-done = bf16[768,2304]{1,0:T(8,128)(2,1)} async-done(((bf16[24,2304]{1,0:T(8,128)(2,1)}), bf16[768,2304]{1,0:T(8,128)(2,1)}) %all-gather.5.cloned.1.call-update) | async-done | bytes 3538960 | tf_op jit(solution)/shard_map/all_gather | solution.py:55
  94.1 8.7 pad_maximum_fusion
  108.6 57.9 %all_gather.51 = s32[2,2048]{1,0:T(2,128)S(1)} all-gather(s32[2,512]{1,0:T(2,128)S(1)} %copy-done.46), channel_id=1, replica_groups=mesh['seq'=4,'fsdp'=8] {'seq'}, dimensions={1}, use_global_device_ids=true | all-gather | bytes 20480 | tf_op jit(solution)/shard_map/all_gather | solution.py:89
  186.0 213.2 %while.69 = (s32[]{:T(128)}, bf16[8,512,3,64]{1,3,2,0:T(8,128)(2,1)S(1)}, f32[8,3,512]{2,1,0:T(4,128)S(1)}, s32[8]{0:T(128)S(1)}, bf16[2,2048,3,64]{1,3,2,0:T(8,...) while((s32[]{:T(128)}, ...), condition=%wide.region_5.6_spmd.clone, body=%wide.region_2.5_spmd.clone.sunk | while | flops 846298112 | bytes 44003840 | solution.py:145
  190.3 8.7 fusion.133
  199.0 6.8 fusion.134
  205.8 7.1 fusion.135
  217.2 8.4 fusion.133
  225.7 6.8 fusion.134
  232.4 7.0 fusion.135
  243.8 8.4 fusion.133
  252.2 6.8 fusion.134
  259.0 7.6 fusion.135
  271.0 8.4 fusion.133
  279.3 6.8 fusion.134
  286.1 7.0 fusion.135
  297.5 8.4 fusion.133
  305.9 6.8 fusion.134
  312.6 7.0 fusion.135
  324.0 8.4 fusion.133
  332.4 6.8 fusion.134
  339.1 7.0 fusion.135
  350.5 8.4 fusion.133
  358.9 6.8 fusion.134
  365.7 7.0 fusion.135
  377.0 8.4 fusion.133
  385.4 6.8 fusion.134
  392.2 7.0 fusion.135
  403.3 6.5 copy.126
  413.8 24.5 %all-to-all-done.1 = bf16[2,2048,192]{2,0,1:T(2,128)(2,1)S(1)} async-done(((bf16[2,2048,192]{2,0,1:T(2,128)(2,1)}), bf16[2,2048,192]{2,0,1:T(2,128)(2,1)S(1)}, u32[]{:S(2)}, u32[]{:S(2)}) %all-to-all-start.1) | async-done | bytes 1572896 | tf_op jit(solution)/shard_map/all_to_all | solution.py:149
  439.7 9.4 copy.127
  456.3 11.0 fusion.81
  467.3 18.6 %convert_reduce_fusion = (f32[3072]{0:T(1024)}, bf16[1024,3072]{1,0:T(8,128)(2,1)S(1)}) fusion(bf16[1024,768]{1,0:T(8,128)(2,1)} %bitcast.236, bf16[3072,768]{1,0:T(8,128)(2,1)} %all-gather.11.cloned.1.call-done, f32[1024,3072]{1,0:T(8,128)} %fusion.81, f32[3072]{0:T(1024)S(1)} %convert_element_type.133), kind=kOutput, calls=%fused_computation.77 | convolution fusion | flops 4916769792 | bytes 25190400 | tf_op jit(solution)/shard_map/nd,fd->nf/dot_general | solution.py:179
  485.9 6.1 multiply_reduce_fusion.1
  499.3 10.6 fusion.80
  520.8 13.0 %fusion.82 = f32[3072,768]{1,0:T(8,128)} fusion(bf16[1024,768]{1,0:T(8,128)(2,1)S(1)} %bitcast.237, f32[1024,3072]{1,0:T(8,128)} %fusion.81, f32[3072]{0:T(1024)S(1)} %convert_element_type.133), kind=kOutput, calls=%fused_computation.137 | convolution fusion | flops 4863295488 | bytes 23605248 | tf_op jit(solution)/shard_map/nf,nd->fd/dot_general | solution.py:176
  542.1 308.2 %while.71 = (s32[]{:T(128)}, bf16[2,2048,3,64]{1,3,2,0:T(8,128)(2,1)}, bf16[2,2048,3,64]{1,3,2,0:T(8,128)(2,1)}, bf16[2,2048,3,64]{1,3,2,0:T(8,128)(2,1)}, s32[2...) while((s32[]{:T(128)}, ...), condition=%wide.region_14.15_spmd.clone, body=%wide.region_10.14_spmd.clone.sunk | while | flops 2065660928 | bytes 185041104 | solution.py:247
  549.3 135.8 %while.72 = (s32[]{:T(128)}, f32[2048,3,64]{0,2,1:T(8,128)}, f32[2048,3,64]{0,2,1:T(8,128)}, bf16[4,512,3,64]{1,3,2,0:T(8,128)(2,1)}, s32[4]{0:T(128)S(1)}, /*in...) while((s32[]{:T(128)}, f32[2048,3,64]{0,2,1:T(8,128)}, ...), condition=%wide.region_13.13_spmd.clone, body=%wide.region_11.12_spmd.clone.sunk | while | flops 2065660928 | bytes 150412816 | solution.py:242
  566.0 6.1 multiply_convert_fusion.5
  599.8 6.1 multiply_convert_fusion.5
  622.4 6.2 fusion.147
  634.4 6.1 multiply_convert_fusion.5
  640.6 6.1 fusion.148
  669.0 6.1 multiply_convert_fusion.5
  703.0 136.4 %while.72 = (s32[]{:T(128)}, f32[2048,3,64]{0,2,1:T(8,128)}, f32[2048,3,64]{0,2,1:T(8,128)}, bf16[4,512,3,64]{1,3,2,0:T(8,128)(2,1)}, s32[4]{0:T(128)S(1)}, /*in...) while((s32[]{:T(128)}, f32[2048,3,64]{0,2,1:T(8,128)}, ...), condition=%wide.region_13.13_spmd.clone, body=%wide.region_11.12_spmd.clone.sunk | while | flops 2065660928 | bytes 150412816 | solution.py:242
  719.7 6.1 multiply_convert_fusion.5
  753.4 6.1 multiply_convert_fusion.5
  759.5 6.1 fusion.148
  776.2 6.2 fusion.147
  788.2 6.1 multiply_convert_fusion.5
  794.3 6.6 fusion.148
  811.3 6.1 fusion.147
  823.2 6.1 multiply_convert_fusion.5
  855.3 16.1 %copy.134 = bf16[3,2,2048,192]{3,1,0,2:T(2,128)(2,1)} copy(bf16[3,2,2048,192]{2,3,1,0:T(8,128)(2,1)} %pad_maximum_fusion.1) | data formatting | bytes 9437184 | tf_op jit(solution)/shard_map/stack | solution.py:251
  877.6 67.7 %all-to-all-done.3 = bf16[3,2,2048,192]{3,1,0,2:T(2,128)(2,1)} async-done(((bf16[3,2,2048,192]{3,1,0,2:T(2,128)(2,1)}), bf16[3,2,2048,192]{3,1,0,2:T(2,128)(2,1)}, u32[]{:S(2)}, u32[]{:S(2)}) %all-to-all-start.3) | async-done | bytes 4718624 | tf_op jit(solution)/shard_map/all_to_all | solution.py:255
  945.3 16.9 %copy.144 = bf16[3,2,4,512,192]{3,2,4,1,0:T(4,128)(2,1)} copy(bf16[3,2,4,512,192]{4,1,0,3,2:T(2,128)(2,1)} %bitcast.17) | data formatting | bytes 9437184 | tf_op jit(solution)/shard_map/all_to_all | solution.py:255
  962.2 9.3 copy.136
  971.5 8.7 reshape.403
  980.2 8.3 fusion.88
  996.0 14.0 %add_convert_fusion.1 = bf16[1024,768]{1,0:T(8,128)(2,1)} fusion(f32[1024,768]{1,0:T(8,128)} %copy-done.10, bf16[3072,768]{1,0:T(8,128)(2,1)} %all-gather.11.cloned.1.call-done, f32[768]{0:T(1024)S(1)} %convert_element_type.135, f32[1024,3072]{1,0:T(8,128)} %fusion.81, f32[3072]{0:T(1024)S(1)} %copy-done.43), kind=kOutput, calls=%fused_computation.117 | convolution fusion | flops 4865654784 | bytes 22035456 | tf_op jit(solution)/shard_map/dot_general | solution.py:164
  1013.6 7.4 bitcast_reduce_fusion
  1024.3 40.8 %all-reduce.18 = (f32[768]{0:T(1024)S(1)}, f32[768]{0:T(1024)S(1)}, f32[768]{0:T(1024)S(1)}, f32[768]{0:T(1024)S(1)}, f32[768]{0:T(1024)S(1)}, /*index=5*/f32[76...) all-reduce(f32[768]{0:T(1024)S(1)} %reduce_sum.223, ...), channel_id=3, replica_groups=mesh['seq'=4,'fsdp'=8] {'seq','fsdp'}, use_global_device_ids=true, to_apply=%region_19.20.clone | all-reduce | flops 9216 | bytes 73728
  1074.9 31.4 %reduce-scatter.5.cloned.1.call-done = f32[24,2304]{1,0:T(8,128)} async-done(((f32[768,2304]{1,0:T(8,128)}), f32[24,2304]{1,0:T(8,128)}) %reduce-scatter.5.cloned.1.call-update) | async-done | bytes 221200 | tf_op jit(solution)/shard_map/reduce_scatter | solution.py:271
  (497 shorter events, 351.5 us)
Async XLA Ops:
  7.2 52.2 %copy-start.7 = (bf16[2,512,768]{2,1,0:T(8,128)(2,1)S(1)}, bf16[2,512,768]{2,1,0:T(8,128)(2,1)}, u32[]{:S(2)}) copy-start(bf16[2,512,768]{2,1,0:T(8,128)(2,1)} %param.22) | copy-start | bytes 4718596
  7.2 6.7 copy-start.54
  7.2 6.9 copy-start.55
  7.2 7.1 copy-start.56
  7.2 7.4 copy-start.57
  7.2 7.6 copy-start.58
  7.2 7.8 copy-start.59
  7.3 8.1 copy-start.60
  7.3 8.3 copy-start.61
  7.3 8.5 copy-start.62
  7.3 66.9 %all-gather.5.cloned.1.call-start = ((), (), s32[]{:S(2)}) async-start(), calls=%async_computation.8 | async-start | bytes 3649536 | tf_op jit(solution)/shard_map/all_gather | solution.py:55
  8.0 442.6 %all-gather.7.cloned.1.call-start = ((), (), s32[]{:S(2)}) async-start(), calls=%async_computation.9 | async-start | bytes 1216512 | tf_op jit(solution)/shard_map/all_gather | solution.py:58
  8.8 447.5 %all-gather.9.cloned.1.call-start = ((), (), s32[]{:S(2)}) async-start(), calls=%async_computation.10 | async-start | bytes 4866048 | tf_op jit(solution)/shard_map/all_gather | solution.py:64
  11.2 47.6 %copy-start.32 = (f32[2,512]{1,0:T(2,128)}, f32[2,512]{1,0:T(2,128)S(1)}, u32[]{:S(2)}) copy-start(f32[2,512]{1,0:T(2,128)S(1)} %get-tuple-element.868) | copy-start | bytes 12292
  11.2 68.8 %copy-start.28 = (f32[1,4,2,128]{3,1,2,0:T(4,128)}, f32[1,4,2,128]{3,1,2,0:T(4,128)S(1)}, u32[]{:S(2)}) copy-start(f32[1,4,2,128]{3,1,2,0:T(4,128)S(1)} %copy.164) | copy-start | bytes 12292
  13.9 45.0 %copy-start.38 = (f32[1,4,2,128]{3,1,2,0:T(4,128)}, f32[1,4,2,128]{3,1,2,0:T(4,128)S(1)}, u32[]{:S(2)}) copy-start(f32[1,4,2,128]{3,1,2,0:T(4,128)S(1)} %copy.165) | copy-start | bytes 12292
  13.9 66.2 %copy-start.30 = (f32[1024]{0:T(1024)}, f32[1024]{0:T(1024)S(1)}, u32[]{:S(2)}) copy-start(f32[1024]{0:T(1024)S(1)} %rsqrt.23) | copy-start | bytes 12292
  102.9 63.6 %all-to-all-start = ((bf16[3,2,512,768]{2,1,0,3:T(2,128)(2,1)}), bf16[3,2,512,768]{2,1,0,3:T(2,128)(2,1)}, u32[]{:S(2)}, u32[]{:S(2)}) async-start(bf16[3,2,512,768]{2,1,0,3:T(2,128)(2,1)} %pad_maximum_fusion), calls=%async_computation | async-start | bytes 9437184 | tf_op jit(solution)/shard_map/all_to_all | solution.py:109
  108.0 359.3 %all-gather.11.cloned.1.call-start = ((), (), s32[]{:S(2)}) async-start(), calls=%async_computation.11 | async-start | bytes 4866048 | tf_op jit(solution)/shard_map/all_gather | solution.py:66
  403.2 10.5 copy-start.52
  403.2 10.5 copy-start.51
  403.3 10.5 copy-start.50
  403.3 10.5 copy-start.45
  409.7 28.6 %all-to-all-start.1 = ((bf16[2,2048,192]{2,0,1:T(2,128)(2,1)}), bf16[2,2048,192]{2,0,1:T(2,128)(2,1)S(1)}, u32[]{:S(2)}, u32[]{:S(2)}) async-start(bf16[2,2048,192]{2,0,1:T(2,128)(2,1)} %copy.126), calls=%async_computation.1 | async-start | bytes 4194304 | tf_op jit(solution)/shard_map/all_to_all | solution.py:149
  413.7 661.1 %reduce-scatter.7.cloned.1.call-start = ((), (), s32[]{:S(2)}) async-start(), calls=%async_computation.13 | async-start | bytes 2433024 | tf_op jit(solution)/shard_map/reduce_scatter | solution.py:274
  413.8 107.0 %copy-start.42 = (f32[3072]{0:T(1024)}, f32[3072]{0:T(1024)S(1)}, u32[]{:S(2)}) copy-start(f32[3072]{0:T(1024)S(1)} %convert_element_type.133) | copy-start | bytes 36868
  439.7 11.0 copy-start.8
  467.3 18.6 %copy-start.11 = (f32[1024,768]{1,0:T(8,128)S(1)}, f32[1024,768]{1,0:T(8,128)}, u32[]{:S(2)}) copy-start(f32[1024,768]{1,0:T(8,128)} %copy-done.10) | copy-start | bytes 9437188
  467.3 18.6 %copy-start.53 = (bf16[768,3072]{1,0:T(8,128)(2,1)S(1)}, bf16[768,3072]{1,0:T(8,128)(2,1)}, u32[]{:S(2)}) copy-start(bf16[768,3072]{1,0:T(8,128)(2,1)} %all-gather.9.cloned.1.call-done) | copy-start | bytes 14155780
  485.9 6.1 copy-start.20
  499.3 575.6 %reduce-scatter.9.cloned.1.call-start = ((), (), s32[]{:S(2)}) async-start(), calls=%async_computation.14 | async-start | bytes 9732096 | tf_op jit(solution)/shard_map/reduce_scatter | solution.py:280
  514.1 6.7 copy-start.16
  517.2 22.2 %all-to-all-start.2 = ((bf16[2,512,768]{1,0,2:T(2,128)(2,1)}), bf16[2,512,768]{1,0,2:T(2,128)(2,1)S(1)}, u32[]{:S(2)}, u32[]{:S(2)}) async-start(bf16[2,512,768]{1,0,2:T(2,128)(2,1)} %copy.128), calls=%async_computation.2 | async-start | bytes 3145728 | tf_op jit(solution)/shard_map/all_to_all | solution.py:201
  520.7 554.1 %reduce-scatter.11.cloned.1.call-start = ((), (), s32[]{:S(2)}) async-start(), calls=%async_computation.15 | async-start | bytes 9732096 | tf_op jit(solution)/shard_map/reduce_scatter | solution.py:282
  542.5 6.8 copy-start.13
  549.3 6.2 copy-start.2
  549.3 6.2 copy-start.5
  581.6 6.2 copy-start.2
  581.6 6.2 copy-start.5
  605.9 6.0 copy-start
  616.1 6.3 copy-start.2
  616.1 6.3 copy-start.5
  640.6 6.1 copy-start
  650.9 6.2 copy-start.2
  650.9 6.2 copy-start.5
  675.1 5.9 copy-start
  685.1 7.9 copy-start.4
  696.0 6.9 copy-start.13
  703.0 6.2 copy-start.2
  703.0 6.2 copy-start.5
  735.3 6.2 copy-start.2
  735.3 6.2 copy-start.5
  759.5 6.1 copy-start
  769.9 6.3 copy-start.2
  769.9 6.3 copy-start.5
  794.3 6.6 copy-start
  805.1 6.2 copy-start.2
  805.1 6.2 copy-start.5
  839.3 7.9 copy-start.4
  871.4 73.8 %all-to-all-start.3 = ((bf16[3,2,2048,192]{3,1,0,2:T(2,128)(2,1)}), bf16[3,2,2048,192]{3,1,0,2:T(2,128)(2,1)}, u32[]{:S(2)}, u32[]{:S(2)}) async-start(bf16[3,2,2048,192]{3,1,0,2:T(2,128)(2,1)} %copy.134), calls=%async_computation.3 | async-start | bytes 12582912 | tf_op jit(solution)/shard_map/all_to_all | solution.py:255
  876.9 229.4 %reduce-scatter.5.cloned.1.call-start = ((), (), s32[]{:S(2)}) async-start(), calls=%async_computation.12 | async-start | bytes 7299072 | tf_op jit(solution)/shard_map/reduce_scatter | solution.py:271
  1013.6 7.5 copy-start.39
  1013.6 9.0 copy-start.31
  1021.1 49.3 %copy-start.37 = (f32[1024]{0:T(1024)S(1)}, f32[1024]{0:T(1024)}, u32[]{:S(2)}) copy-start(f32[1024]{0:T(1024)} %copy-done.36) | copy-start | bytes 12292
  (60 other events, 203.8 us)
Sparse Core Ops, SparseCore 0:
  11.1 63.0 all-gather.4
  77.2 71.6 all-gather.6
  151.9 62.5 all-gather.8
  217.5 62.4 all-gather.10
  499.4 97.2 reduce-scatter.6
  604.0 134.6 reduce-scatter.8
  745.2 134.6 reduce-scatter.10
  988.6 117.6 reduce-scatter.4
where the time goes:
time: 1130 us; the launch traced here: 1110 us
  matrix products  426 us (38%)
  local copies, waits for them, and re-layouts  174 us (15%)
  other arithmetic  153 us (14%)
  waiting for transfers between devices  146 us (13%)
  blocking collectives  141 us (12%)
  loops' own time  38.5 us (3%)
  starting transfers between devices  18.4 us (2%)
  between operations  15.2 us (1%)
    dot_general x16, matrix products, block_scores(): jnp.einsum('qhd,khd->hqk', query_block, key_all, preferred_element_type=j...  92.9 us
    unnamed x2, blocking collectives  83.5 us
    all_to_all x1, waiting for transfers between devices, body(): lax.all_to_all(grad_packed, 'seq', split_axis=2, concat_axis=3, tiled=True)  67.7 us
    all_gather x1, blocking collectives, body(): whole_segments = lax.all_gather(segments, 'seq', axis=1, tiled=True)  57.9 us
    dot_general x8, matrix products, forward_block(): jnp.einsum('hqk,khd->qhd', soft_probs, value_all, preferred_element_type=...  56.5 us
    reduce_sum x8, other arithmetic, forward_block(): row_total = jnp.sum(shifted, axis=-1, keepdims=True)  54.2 us
    convert_element_type x8, other arithmetic, back_step(): score_low = score_grad.astype(jnp.bfloat16)  49 us
    dot_general x8, matrix products, back_step(): jnp.einsum('hqk,khd->qhd', score_low, key_all, preferred_element_type=jnp...  48.3 us
  transfers between devices with their start and end apart: 12, of which 5 were waited for; matrix products, arithmetic and copies ran while one was open for 64% of the time, Pallas kernels for 0%

commit v1 on v0

v1 whole, which is shorter than its diff:
```python
import functools

import jax
import jax.numpy as jnp
from jax import lax
from jax.experimental import pallas as pl
from jax.experimental.pallas import tpu as pltpu
from jax.sharding import PartitionSpec as P

HD = 64
NORM_EPS = 1e-05
NEG = -1e30
B = 256
MOST_DOC = 1024
ALL = ("seq", "fsdp")
BF = jnp.bfloat16
F32 = jnp.float32
NT = (((1,), (1,)), ((), ()))
NN = (((1,), (0,)), ((), ()))
TN = (((0,), (0,)), ((), ()))


def dg(a, b, dims):
    return lax.dot_general(a, b, dims, preferred_element_type=F32)


def fwd_kernel(lo_ref, start_ref, q_ref, k_ref, v_ref, o_ref, lse_ref, qm, vt, sbuf, mx8, *, heads):
    n = q_ref.shape[0] // B
    lane = lax.broadcasted_iota(jnp.int32, (B, 128), 1)
    kio = lax.broadcasted_iota(jnp.int32, (B, B), 0)
    qio = lax.broadcasted_iota(jnp.int32, (B, B), 1)

    def transpose_block(j, _):
        s = pl.ds(pl.multiple_of(j * B, B), B)
        for p in range(heads // 2):
            vt[128 * p : 128 * p + 128, s] = v_ref[s, 128 * p : 128 * p + 128].T
        return 0

    lax.fori_loop(0, n, transpose_block, 0)

    def qblock(i, _):
        qs = pl.multiple_of(i * B, B)
        for p in range(heads // 2):
            qq = q_ref[pl.ds(qs, B), 128 * p : 128 * p + 128]
            qm[2 * p] = jnp.where(lane < 64, qq, jnp.zeros_like(qq))
            qm[2 * p + 1] = jnp.where(lane >= 64, qq, jnp.zeros_like(qq))
        st_row = start_ref[pl.ds(i, 1), :]

        def scores(j, first):
            ks = pl.multiple_of(j * B, B)
            mask = (kio + ks) >= st_row
            if first:
                mask = mask & (kio <= qio)
            slot = i - j
            for h in range(heads):
                p = h // 2
                k_blk = k_ref[pl.ds(ks, B), 128 * p : 128 * p + 128]
                st = jnp.where(mask, dg(k_blk, qm[h], NT), NEG)
                sbuf[h, slot] = st
                m8 = jnp.max(st.reshape(B // 8, 8, B), axis=0)
                mx8[h] = m8 if first else jnp.maximum(mx8[h], m8)

        scores(i, True)

        def score_step(j, c):
            scores(j, False)
            return c

        lax.fori_loop(lo_ref[i], i, score_step, 0)
        ms = [jnp.max(mx8[h], axis=0, keepdims=True) for h in range(heads)]

        def weigh(j):
            ks = pl.multiple_of(j * B, B)
            slot = i - j
            outs = []
            for h in range(heads):
                p = jnp.exp(sbuf[h, slot] - ms[h])
                l8 = jnp.sum(p.reshape(B // 8, 8, B), axis=0)
                ot = dg(vt[64 * h : 64 * h + 64, pl.ds(ks, B)], p.astype(BF), NN)
                outs.append((ot, l8))
            return outs

        def weigh_step(j, c):
            return [(a[0] + b[0], a[1] + b[1]) for a, b in zip(c, weigh(j))]

        res = lax.fori_loop(lo_ref[i], i, weigh_step, weigh(i))
        for p in range(heads // 2):
            rows = []
            for h in (2 * p, 2 * p + 1):
                total = jnp.sum(res[h][1], axis=0, keepdims=True)
                rows.append(res[h][0] * (1.0 / total))
                lse_ref[h : h + 1, pl.ds(qs, B)] = ms[h] + jnp.log(total)
            pair = jnp.concatenate(rows, axis=0)
            o_ref[pl.ds(qs, B), 128 * p : 128 * p + 128] = pair.T.astype(BF)
        return 0

    lax.fori_loop(0, n, qblock, 0)


def attn_fwd(lo, start, q, k, v):
    n, w = q.shape
    heads = w // HD
    maxb = min(n // B, (MOST_DOC + B - 2) // B + 1)
    return pl.pallas_call(
        functools.partial(fwd_kernel, heads=heads),
        out_shape=(jax.ShapeDtypeStruct((n, w), BF), jax.ShapeDtypeStruct((8, n), F32)),
        in_specs=[pl.BlockSpec(memory_space=pltpu.SMEM)]
        + [pl.BlockSpec(memory_space=pltpu.VMEM)] * 4,
        out_specs=[pl.BlockSpec(memory_space=pltpu.VMEM)] * 2,
        scratch_shapes=[
            pltpu.VMEM((heads, B, 128), BF),
            pltpu.VMEM((w, n), BF),
            pltpu.VMEM((heads, maxb, B, B), F32),
            pltpu.VMEM((heads, 8, B), F32),
        ],
        compiler_params=pltpu.CompilerParams(vmem_limit_bytes=32 * 2**20),
        cost_estimate=pl.CostEstimate(
            flops=20_000_000_000, bytes_accessed=6_000_000, transcendentals=0
        ),
        name="attn_fwd",
    )(lo, start, q, k, v)


def bwd_kernel(
    lo_ref, start_ref, q_ref, k_ref, v_ref, do_ref, o_ref, lse_ref,
    dq_ref, dk_ref, dv_ref, qm, dm, dqa, dka, dva, dd, kt, *, heads,
):
    n = q_ref.shape[0] // B
    lane = lax.broadcasted_iota(jnp.int32, (B, 128), 1)
    kio = lax.broadcasted_iota(jnp.int32, (B, B), 0)
    qio = lax.broadcasted_iota(jnp.int32, (B, B), 1)
    dka[...] = jnp.zeros_like(dka)
    dva[...] = jnp.zeros_like(dva)

    def transpose_block(j, _):
        s = pl.ds(pl.multiple_of(j * B, B), B)
        for p in range(heads // 2):
            kt[128 * p : 128 * p + 128, s] = k_ref[s, 128 * p : 128 * p + 128].T
        return 0

    lax.fori_loop(0, n, transpose_block, 0)

    def qblock(i, _):
        qs = pl.multiple_of(i * B, B)
        for p in range(heads // 2):
            cs = slice(128 * p, 128 * p + 128)
            qq = q_ref[pl.ds(qs, B), cs]
            gg = do_ref[pl.ds(qs, B), cs]
            prod = (o_ref[pl.ds(qs, B), cs].astype(F32) * gg.astype(F32)).T
            dd[2 * p : 2 * p + 1, :] = jnp.sum(prod[:64], axis=0, keepdims=True)
            dd[2 * p + 1 : 2 * p + 2, :] = jnp.sum(prod[64:], axis=0, keepdims=True)
            z = jnp.zeros_like(qq)
            qm[2 * p] = jnp.where(lane < 64, qq, z)
            qm[2 * p + 1] = jnp.where(lane >= 64, qq, z)
            dm[2 * p] = jnp.where(lane < 64, gg, z)
            dm[2 * p + 1] = jnp.where(lane >= 64, gg, z)
        st_row = start_ref[pl.ds(i, 1), :]

        def block(j, first):
            ks = pl.multiple_of(j * B, B)
            mask = (kio + ks) >= st_row
            if first:
                mask = mask & (kio <= qio)
            for p in range(heads // 2):
                cs = slice(128 * p, 128 * p + 128)
                k_blk = k_ref[pl.ds(ks, B), cs]
                v_blk = v_ref[pl.ds(ks, B), cs]
                dvs, dks, dqs = [], [], []
                for h in (2 * p, 2 * p + 1):
                    st = dg(k_blk, qm[h], NT)
                    lse = lse_ref[h : h + 1, pl.ds(qs, B)]
                    pt = jnp.exp(jnp.where(mask, st, NEG) - lse)
                    dp = dg(v_blk, dm[h], NT)
                    ds = pt * (dp - dd[h : h + 1, :])
                    pb = pt.astype(BF)
                    db = ds.astype(BF)
                    dvs.append(dg(pb, dm[h], NN))
                    dks.append(dg(db, qm[h], NN))
                    dqs.append(dg(kt[64 * h : 64 * h + 64, pl.ds(ks, B)], db, NN))
                dva[pl.ds(ks, B), cs] += dvs[0] + dvs[1]
                dka[pl.ds(ks, B), cs] += dks[0] + dks[1]
                dq = jnp.concatenate(dqs, axis=0)
                if first:
                    dqa[cs, :] = dq
                else:
                    dqa[cs, :] += dq

        block(i, True)

        def step(j, c):
            block(j, False)
            return c

        lax.fori_loop(lo_ref[i], i, step, 0)
        for p in range(heads // 2):
            cs = slice(128 * p, 128 * p + 128)
            dq_ref[pl.ds(qs, B), cs] = (dqa[cs, :] * 0.125).T.astype(BF)
        return 0

    lax.fori_loop(0, n, qblock, 0)

    def finish(i, _):
        s = pl.ds(pl.multiple_of(i * B, B), B)
        dk_ref[s, :] = dka[s, :].astype(BF)
        dv_ref[s, :] = dva[s, :].astype(BF)
        return 0

    lax.fori_loop(0, n, finish, 0)


def attn_bwd(lo, start, q, k, v, do, o, lse):
    n, w = q.shape
    heads = w // HD
    s = jax.ShapeDtypeStruct((n, w), BF)
    return pl.pallas_call(
        functools.partial(bwd_kernel, heads=heads),
        out_shape=(s, s, s),
        in_specs=[pl.BlockSpec(memory_space=pltpu.SMEM)]
        + [pl.BlockSpec(memory_space=pltpu.VMEM)] * 7,
        out_specs=[pl.BlockSpec(memory_space=pltpu.VMEM)] * 3,
        scratch_shapes=[
            pltpu.VMEM((heads, B, 128), BF),
            pltpu.VMEM((heads, B, 128), BF),
            pltpu.VMEM((w, B), F32),
            pltpu.VMEM((n, w), F32),
            pltpu.VMEM((n, w), F32),
            pltpu.VMEM((8, B), F32),
            pltpu.VMEM((w, n), BF),
        ],
        compiler_params=pltpu.CompilerParams(vmem_limit_bytes=40 * 2**20),
        cost_estimate=pl.CostEstimate(
            flops=44_000_000_000, bytes_accessed=12_000_000, transcendentals=0
        ),
        name="attn_bwd",
    )(lo, start, q, k, v, do, o, lse)


def pick(array, index, axis=0):
    return lax.dynamic_index_in_dim(array, index, axis, keepdims=False)


def ordered(flag, first, second, axis):
    return jnp.stack(
        [jnp.where(flag == 1, second, first), jnp.where(flag == 1, first, second)], axis
    )


class Net:
    def __init__(self):
        self.nq = lax.axis_size("seq")
        self.nf = lax.axis_size("fsdp")
        self.q = lax.axis_index("seq")
        f = lax.axis_index("fsdp")
        self.z = f // 2
        self.c = f % 2
        self.bits = (self.nf // 2).bit_length() - 1

    def permute(self, value, target):
        pairs = []
        for q in range(self.nq):
            for f in range(self.nf):
                tq, tf = target(q, f)
                pairs.append((q * self.nf + f, tq * self.nf + tf))
        return lax.ppermute(value, ALL, pairs)

    def flip_q(self, value, mask):
        return self.permute(value, lambda q, f: (q ^ mask, f))

    def flip_f(self, value, mask):
        return self.permute(value, lambda q, f: (q, f ^ mask))

    def swap(self, value):
        return self.flip_f(value, 1)

    def _token_target(self, p):
        return lambda q, f: (2 * (f % 2) + (p ^ (q % 2)), (f // 2) * 2 + q // 2)

    def to_chip(self, parts):
        h = self.q % 2
        got = [
            self.permute(jnp.where(h == p, parts[0], parts[1]), self._token_target(p))
            for p in range(2)
        ]
        return jnp.where(h == 0, got[0], got[1]), jnp.where(h == 0, got[1], got[0])

    def from_chip(self, halves):
        h = self.q % 2
        got = []
        for p in range(2):
            forward = self._token_target(p)
            back = {}
            for q in range(self.nq):
                for f in range(self.nf):
                    back[forward(q, f)] = (q, f)
            got.append(
                self.permute(
                    jnp.where(h == p, halves[0], halves[1]), lambda q, f, b=back: b[(q, f)]
                )
            )
        return jnp.stack([jnp.where(h == 0, got[0], got[1]), jnp.where(h == 0, got[1], got[0])])

    def gather_z(self, block):
        out = block[None]
        shape = block.shape
        for level in range(self.bits):
            bit = self.bits - 1 - level
            got = self.flip_f(out, 2 << bit)
            out = ordered((self.z >> bit) & 1, out, got, 1).reshape((-1,) + shape)
        return out

    def scatter_z(self, blocks):
        shape = blocks.shape[1:]
        for bit in range(self.bits):
            parts = blocks.reshape((-1, 2) + shape)
            mine = (self.z >> bit) & 1
            got = self.flip_f(pick(parts, 1 - mine, 1).astype(BF), 2 << bit)
            blocks = pick(parts, mine, 1).astype(F32) + got.astype(F32)
        return blocks[0]

    def gather_q(self, block):
        half = block.shape[0] // 2
        one = self.flip_q(block, 1)
        two = self.flip_q(block, 2)
        three = jnp.concatenate([self.flip_q(one[:half], 2), self.flip_q(two[half:], 1)])
        return [block, one, two, three]

    def absolute(self, blocks):
        shape = blocks[0].shape
        out = jnp.zeros((4,) + shape, blocks[0].dtype)
        for r, block in enumerate(blocks):
            out = lax.dynamic_update_slice(out, block[None], (self.q ^ r,) + (0,) * len(shape))
        return out

    def scatter_q(self, blocks):
        half = blocks.shape[1] // 2
        b1, b2, b3 = (pick(blocks, self.q ^ r).astype(F32) for r in (1, 2, 3))
        far_a = self.flip_q(b3[:half].astype(BF), 2)
        far_b = self.flip_q(b3[half:].astype(BF), 1)
        b1 = jnp.concatenate([b1[:half] + far_a.astype(F32), b1[half:]])
        b2 = jnp.concatenate([b2[:half], b2[half:] + far_b.astype(F32)])
        one = self.flip_q(b1.astype(BF), 1)
        two = self.flip_q(b2.astype(BF), 2)
        return pick(blocks, self.q).astype(F32) + one.astype(F32) + two.astype(F32)


def row_stats(v):
    mean = jnp.mean(v, axis=-1, keepdims=True)
    centered = v - mean
    var = jnp.mean(centered * centered, axis=-1, keepdims=True)
    inv = lax.rsqrt(var + NORM_EPS)
    return centered * inv, inv


def norm_back(xhat, inv, gain, e):
    c = e * gain
    return inv * (
        c
        - jnp.mean(c, axis=-1, keepdims=True)
        - xhat * jnp.mean(c * xhat, axis=-1, keepdims=True)
    )


def body(
    tokens,
    segments,
    qkv_weight,
    query_bias,
    value_bias,
    proj_weight,
    proj_bias,
    attn_gain,
    attn_shift,
    ffn_gain,
    ffn_shift,
    expand_weight,
    expand_bias,
    contract_weight,
    contract_bias,
    cotangent,
):
    net = Net()
    c, z = net.c, net.z
    micro, local, width = tokens.shape
    rows = qkv_weight.shape[0]
    ff = expand_weight.shape[1]
    ff_rows = contract_weight.shape[0]
    ratio = ff // width
    half = width // 2
    nq, nz = net.nq, net.nf // 2
    blk = rows * net.nf
    n = 2 * micro * local
    mine = micro * local

    lanes = width
    seg_rows = jnp.zeros((micro, 8, lanes), BF).at[:, 0, :local].set(segments.astype(BF))
    tok_send = jnp.concatenate([tokens, seg_rows], axis=1)
    t0, t1 = net.to_chip([tok_send[0], tok_send[1]])
    tok = jnp.concatenate([t0[:local], t1[:local]])
    seg_mine = jnp.concatenate([t0[local, :local], t1[local, :local]])

    small = jnp.concatenate(
        [
            query_bias,
            value_bias,
            proj_bias,
            attn_gain,
            attn_shift,
            ffn_gain,
            ffn_shift,
            contract_bias,
            expand_bias,
        ]
    )
    small_len = small.shape[0]
    pad_rows = -(-(3 * rows + 1) // 8) * 8 - 3 * rows
    small_rows = jnp.zeros((pad_rows * half,), BF).at[:small_len].set(small).reshape(pad_rows, half)
    qkv_cut = qkv_weight.reshape(rows, 3, 2, half)
    packs = jnp.stack(
        [
            jnp.concatenate([qkv_cut[:, 0, s], qkv_cut[:, 1, s], qkv_cut[:, 2, s], small_rows])
            for s in range(2)
        ]
    )
    got = net.swap(pick(packs, 1 - c))
    pack = ordered(c, pick(packs, c), got, 0)
    pack = net.gather_z(pack)
    pack = pack.reshape(net.nf * (3 * rows + pad_rows), half)
    pack = net.absolute(net.gather_q(pack)).reshape(nq, net.nf, 3 * rows + pad_rows, half)
    w_qkv = jnp.concatenate(
        [pack[:, :, s * rows : (s + 1) * rows].reshape(width, half) for s in range(3)], axis=1
    )
    vectors = pack[:, :, 3 * rows :].reshape(nq, net.nf, -1)[:, :, :small_len].astype(F32)
    names = []
    for s in range(8):
        names.append(vectors[:, :, s * rows : (s + 1) * rows].reshape(width))
    q_off, v_off, proj_off, a_gain, a_shift, f_gain, f_shift, con_off = names
    exp_off = vectors[:, :, 8 * rows :].reshape(ff)

    proj_cut = proj_weight.reshape(rows, 2, half)
    con_cut = contract_weight.reshape(ff_rows, 2, half)
    exp_cut = expand_weight.reshape(rows, 2, ratio, half)
    packs2 = jnp.stack(
        [
            jnp.concatenate(
                [con_cut[:, s], proj_cut[:, s]] + [exp_cut[:, s, t] for t in range(ratio)]
            )
            for s in range(2)
        ]
    )
    got2 = net.swap(pick(packs2, 1 - c))
    pack2 = ordered(c, pick(packs2, c), got2, 0)
    pack2 = net.gather_z(pack2).reshape(net.nf, -1, half)
    cuts = [ff_rows, ff_rows + rows]
    pieces2 = [pack2[:, : cuts[0]].reshape(-1, half), pack2[:, cuts[0] : cuts[1]].reshape(-1, half)]
    for t in range(ratio):
        pieces2.append(pack2[:, cuts[1] + t * rows : cuts[1] + (t + 1) * rows].reshape(-1, half))
    pack2 = jnp.concatenate(pieces2)
    quarters = net.gather_q(pack2)
    others = [net.swap(x) for x in quarters]
    own_half = net.absolute(quarters)
    other_half = net.absolute(others)
    w_left = jnp.where(c == 0, own_half, other_half)
    w_right = jnp.where(c == 0, other_half, own_half)
    n_con, n_proj = ratio * blk, blk
    w_con = jnp.concatenate(
        [w_left[:, :n_con].reshape(ff, half), w_right[:, :n_con].reshape(ff, half)], axis=1
    )
    w_proj = jnp.concatenate(
        [
            w_left[:, n_con : n_con + n_proj].reshape(width, half),
            w_right[:, n_con : n_con + n_proj].reshape(width, half),
        ],
        axis=1,
    )
    w_exp = jnp.concatenate(
        [
            x[:, n_con + n_proj + t * blk : n_con + n_proj + (t + 1) * blk].reshape(width, half)
            for x in (w_left, w_right)
            for t in range(ratio)
        ],
        axis=1,
    )

    tok32 = tok.astype(F32)
    xhat_one, inv_one = row_stats(tok32)
    normed = (xhat_one * a_gain + a_shift).astype(BF)
    seg_row = jnp.zeros((16, width), BF).at[:2, :local].set(seg_mine.reshape(2, local))
    both = ordered(c, jnp.concatenate([normed, seg_row]), net.swap(jnp.concatenate([normed, seg_row])), 0)
    normed_all = both[:, :mine].reshape(n, width)
    seg = both[:, mine : mine + 2, :local].reshape(n).astype(jnp.int32)
    docs = jnp.arange(32, dtype=jnp.int32)
    before = jnp.sum((seg[None, :] < docs[:, None]).astype(jnp.int32), axis=1)
    start = jnp.sum(jnp.where(seg[None, :] == docs[:, None], before[:, None], 0), axis=0)
    lo = start[::B] // B
    start = start.reshape(n // B, B)
    mixed = dg(normed_all, w_qkv, NN)
    q_half = pick(q_off.reshape(2, half), c)
    v_half = pick(v_off.reshape(2, half), c)
    query = (mixed[:, :half] + q_half).astype(BF) * BF(0.125)
    key = mixed[:, half : 2 * half].astype(BF)
    value = (mixed[:, 2 * half :] + v_half).astype(BF)
    att, lse = attn_fwd(lo, start, query, key, value)

    att_cut = att.reshape(2, mine, half)
    att_own, att_got = pick(att_cut, c), net.swap(pick(att_cut, 1 - c))
    attended = jnp.concatenate(
        [jnp.where(c == 0, att_own, att_got), jnp.where(c == 0, att_got, att_own)], axis=1
    )
    middle = tok32 + (dg(attended, w_proj, NN) + proj_off)
    xhat_two, inv_two = row_stats(middle)
    normed_two = (xhat_two * f_gain + f_shift).astype(BF)
    hidden = dg(normed_two, w_exp, NN) + exp_off
    inner = 0.7978845608028654 * (hidden + 0.044715 * hidden * hidden * hidden)
    th = jnp.tanh(inner)
    active = (0.5 * hidden * (1.0 + th)).astype(BF)
    slope = 0.5 * (1.0 + th) + 0.5 * hidden * (1.0 - th * th) * (
        0.7978845608028654 * (1.0 + 3 * 0.044715 * hidden * hidden)
    )
    out = (middle + (dg(active, w_con, NN) + con_off)).astype(BF)
    result = net.from_chip([out[:local], out[local:]])

    g0, g1 = net.to_chip([cotangent[0], cotangent[1]])
    g = jnp.concatenate([g0, g1])
    g32 = g.astype(F32)
    con_off_grad = jnp.sum(g32, axis=0)
    con_grad = dg(active, g, TN)
    hidden_grad = (dg(g, w_con, NT) * slope).astype(BF)
    exp_off_grad = jnp.sum(hidden_grad.astype(F32), axis=0)
    exp_grad = dg(normed_two, hidden_grad, TN)
    e_two = dg(hidden_grad, w_exp, NT)
    f_gain_grad = jnp.sum(e_two * xhat_two, axis=0)
    f_shift_grad = jnp.sum(e_two, axis=0)
    middle_grad = g32 + norm_back(xhat_two, inv_two, f_gain, e_two)
    branch = middle_grad.astype(BF)
    proj_off_grad = jnp.sum(branch.astype(F32), axis=0)
    proj_grad = dg(attended, branch, TN)
    att_grad = dg(branch, w_proj, NT).astype(BF)
    ag_cut = att_grad.reshape(mine, 2, half)
    ag_own, ag_got = pick(ag_cut, c, 1), net.swap(pick(ag_cut, 1 - c, 1))
    grad_heads = ordered(c, ag_own, ag_got, 0).reshape(n, half)

    con_g = con_grad.reshape(nq, n_con, 2, half)
    proj_g = proj_grad.reshape(nq, n_proj, 2, half)
    exp_g = exp_grad.reshape(nq, blk, 2, ratio, half)

    def half_pack(s):
        return jnp.concatenate(
            [pick(con_g, s, 2), pick(proj_g, s, 2)]
            + [pick(exp_g, s, 2)[:, :, t] for t in range(ratio)],
            axis=1,
        )

    summed = half_pack(c) + net.swap(half_pack(1 - c).astype(BF)).astype(F32)
    summed = net.scatter_q(summed)
    per_f = jnp.concatenate(
        [
            summed[:n_con].reshape(net.nf, ff_rows, half),
            summed[n_con : n_con + n_proj].reshape(net.nf, rows, half),
        ]
        + [
            summed[n_con + n_proj + t * blk : n_con + n_proj + (t + 1) * blk].reshape(
                net.nf, rows, half
            )
            for t in range(ratio)
        ],
        axis=1,
    )
    per_core = net.scatter_z(per_f.reshape(nz, 2, -1, half))
    kept = pick(per_core, c)
    final = ordered(c, kept, net.swap(pick(per_core, 1 - c)), 0)
    con_out = jnp.concatenate([final[0, :ff_rows], final[1, :ff_rows]], axis=1)
    proj_out = jnp.concatenate([final[0, ff_rows : ff_rows + rows], final[1, ff_rows : ff_rows + rows]], axis=1)
    exp_out = jnp.concatenate(
        [
            final[s, ff_rows + rows + t * rows : ff_rows + rows + (t + 1) * rows]
            for s in range(2)
            for t in range(ratio)
        ],
        axis=1,
    )

    dq, dk, dv = attn_bwd(lo, start, query, key, value, grad_heads, att, lse)
    d_mixed = jnp.concatenate([dq, dk, dv], axis=1)
    q_off_half = jnp.sum(dq.astype(F32), axis=0)
    v_off_half = jnp.sum(dv.astype(F32), axis=0)
    qkv_grad = dg(normed_all, d_mixed, TN)
    e_part = dg(d_mixed, w_qkv, NT).reshape(2, mine, width)
    e_one = pick(e_part, c) + net.swap(pick(e_part, 1 - c).astype(BF)).astype(F32)
    a_gain_grad = jnp.sum(e_one * xhat_one, axis=0)
    a_shift_grad = jnp.sum(e_one, axis=0)
    tok_grad = (middle_grad + norm_back(xhat_one, inv_one, a_gain, e_one)).astype(BF)
    token_grad = net.from_chip([tok_grad[:local], tok_grad[local:]])

    qkv_g = jnp.concatenate(
        [qkv_grad[:, s * half : (s + 1) * half].reshape(nq, blk, half) for s in range(3)], axis=1
    )
    qkv_sum = net.scatter_q(qkv_g).reshape(3, net.nf, rows, half).transpose(1, 0, 2, 3)
    qkv_core = net.scatter_z(qkv_sum.reshape(nz, 2, 3 * rows, half))
    qkv_final = ordered(c, pick(qkv_core, c), net.swap(pick(qkv_core, 1 - c)), 0)
    qkv_out = jnp.concatenate(
        [qkv_final[s, t * rows : (t + 1) * rows] for t in range(3) for s in range(2)], axis=1
    )

    zero = jnp.zeros((half,), F32)
    q_off_grad = jnp.where(c == 0, jnp.concatenate([q_off_half, zero]), jnp.concatenate([zero, q_off_half]))
    v_off_grad = jnp.where(c == 0, jnp.concatenate([v_off_half, zero]), jnp.concatenate([zero, v_off_half]))
    parts = [
        x.reshape(nq, net.nf, -1)
        for x in (
            q_off_grad,
            v_off_grad,
            proj_off_grad,
            a_gain_grad,
            a_shift_grad,
            f_gain_grad,
            f_shift_grad,
            con_off_grad,
            exp_off_grad,
        )
    ]
    vec = jnp.concatenate(parts, axis=2)
    for bit in range(2):
        b = (net.q >> bit) & 1
        pairs = vec.reshape(-1, 2, net.nf, small_len)
        vec = pick(pairs, b, 1) + net.flip_q(pick(pairs, 1 - b, 1), 1 << bit)
    vec = vec[0]
    f = 2 * z + c
    for bit in range(net.bits + 1):
        b = (f >> bit) & 1
        pairs = vec.reshape(-1, 2, small_len)
        vec = pick(pairs, b, 1) + net.flip_f(pick(pairs, 1 - b, 1), 1 << bit)
    vec = vec[0]
    outs = [vec[s * rows : (s + 1) * rows] for s in range(8)]
    exp_off_out = vec[8 * rows :]
    return (
        result,
        token_grad,
        qkv_out,
        outs[0],
        outs[1],
        proj_out,
        outs[2],
        outs[3],
        outs[4],
        outs[5],
        outs[6],
        exp_out,
        exp_off_out,
        con_out,
        outs[7],
    )


def solution(mesh):
    act = P("fsdp", "seq", None)
    mat = P(ALL, None)
    vec = P(ALL)
    return jax.shard_map(
        body,
        mesh=mesh,
        in_specs=(
            act, P("fsdp", "seq"), mat, vec, vec, mat, vec, vec, vec, vec, vec, mat, vec, mat, vec, act,
        ),
        out_specs=(act, act, mat, vec, vec, mat, vec, vec, vec, vec, vec, mat, vec, mat, vec),
        check_vma=False,
    )
```

time: 1130 us -> 557 us (0.49); the launches traced: 1110 us -> 552 us
  matrix products: 426 us -> 77.5 us
  blocking collectives: 141 us -> 0 us
  other arithmetic: 153 us -> 74.3 us
  Pallas kernels: 0 us -> 60.3 us
  loops' own time: 38.5 us -> 0 us
  starting transfers between devices: 18.4 us -> 56 us
  waiting for transfers between devices: 146 us -> 116 us
  between operations: 15.2 us -> 3.24 us
    dot_general x68 -> x12, matrix products: 426 us -> 77.5 us  [dg(): return lax.dot_general(a, b, dims, preferred_element_type=F32)]
    ppermute x0 -> x50, waiting for transfers between devices: none -> 116 us  [permute(): return lax.ppermute(value, ALL, pairs)]
    all_to_all x4 -> x0, waiting for transfers between devices: 97.7 us -> none  [the longest x1 67.7 us: body(): lax.all_to_all(grad_packed, 'seq', split_axis=2, concat_axis=3, tiled=True)]
    unnamed x2 -> x0, blocking collectives: 83.5 us -> none
    pallas_call x0 -> x2, Pallas kernels: none -> 60.3 us  [the longest x1 40.4 us: attn_bwd(): pl.pallas_call(functools.partial(bwd_kernel, heads=heads), out_shape=(s,...]
    all_gather x1 -> x0, blocking collectives: 57.9 us -> none  [body(): whole_segments = lax.all_gather(segments, 'seq', axis=1, tiled=True)]
    ppermute x0 -> x50, starting transfers between devices: none -> 56 us  [permute(): return lax.ppermute(value, ALL, pairs)]
    reduce_sum x16 -> x9, other arithmetic: 66.1 us -> 10.3 us  [the longest x1 5.65 us: body(): a_gain_grad = jnp.sum(e_one * xhat_one, axis=0)]
  transfers between devices with their start and end apart: 12 -> 50, of which waited for: 5 -> 18; matrix products, arithmetic and copies ran while one was open for 64% -> 27% of each run, Pallas kernels for 0% -> 11%
where the time goes in v1:
time: 557 us; the launch traced here: 552 us
  local copies, waits for them, and re-layouts  164 us (29%)
  waiting for transfers between devices  116 us (21%)
  matrix products  77.5 us (14%)
  other arithmetic  74.3 us (13%)
  Pallas kernels  60.3 us (11%)
  starting transfers between devices  56 us (10%)
    ppermute x50, waiting for transfers between devices, permute(): return lax.ppermute(value, ALL, pairs)  116 us
    dot_general x12, matrix products, dg(): return lax.dot_general(a, b, dims, preferred_element_type=F32)  77.5 us
    ppermute x50, starting transfers between devices, permute(): return lax.ppermute(value, ALL, pairs)  56 us
    pallas_call x1, Pallas kernels, attn_bwd(): pl.pallas_call(functools.partial(bwd_kernel, heads=heads), out_shape=(s,...  40.4 us
    dynamic_slice x14, local copies, waits for them, and re-layouts, pick(): return lax.dynamic_index_in_dim(array, index, axis, keepdims=False)  33.9 us
    unnamed x223, local copies, waits for them, and re-layouts  29.9 us
    dynamic_update_slice x11, local copies, waits for them, and re-layouts, absolute(): lax.dynamic_update_slice(out, block[None], (self.q ^ r,) + (0,) * len(sha...  21 us
    pallas_call x1, Pallas kernels, attn_fwd(): pl.pallas_call(functools.partial(fwd_kernel, heads=heads), out_shape=(jax...  19.9 us
  transfers between devices with their start and end apart: 50, of which 18 were waited for; matrix products, arithmetic and copies ran while one was open for 27% of the time, Pallas kernels for 11%

profile of v1, /device:TPU:0, one launch (start us, length us, event | category | flops | bytes accessed | tf_op | source)
XLA Modules:
  0.0 551.7 jit_solution(9004502945912745366)
XLA Ops:
  0.7 6.2 %concatenate.154 = bf16[288]{0:T(512)(128)(2,1)S(1)} concatenate(bf16[24]{0:T(256)(128)(2,1)} %param.25, bf16[24]{0:T(256)(128)(2,1)} %param.26, bf16[24]{0:T(256)(128)(2,1)} %param.28, bf16[24]{0:T(256)(128)(2,1)} %param.29, bf16[24]{0:T(256)(128)(2,1)} %param.30, bf16[24]{0:T(256)(128)(2,1)} %param.31, bf16[24]{0:T(256)(128)(2,1)} %param.32, bf16[24]{0:T(256)(128)(2,1)} %param.36, ...), dimensions={0} | concatenate | bytes 1152 | tf_op jit(solution)/shard_map/concatenate | solution.py:401
  16.7 2.9 collective-permute-start.1
  20.5 2.7 collective-permute-start.3
  24.5 7.6 %collective-permute-start.24 = (bf16[512,768]{1,0:T(8,128)(2,1)}, bf16[512,768]{1,0:T(8,128)(2,1)}, u32[]{:S(2)}, u32[]{:S(2)}) collective-permute-start(bf16[512,768]{1,0:T(8,128)(2,1)} %get-tuple-element.274), channel_id=1, source_target_pairs={{0,0},{1,16},{2,2},{3,18},{4,4},{5,20},{6,6},{7,22},{8,8},{9,24},{... | collective-permute-start | bytes 2359304 | tf_op jit(solution)/shard_map/ppermute | solution.py:264
  35.5 3.6 collective-permute-done.4
  43.2 12.3 %collective-permute-done.12 = bf16[1,2,216,384]{3,2,1,0:T(8,128)(2,1)S(1)} collective-permute-done((bf16[1,2,216,384]{3,2,1,0:T(8,128)(2,1)S(1)}, bf16[1,2,216,384]{3,2,1,0:T(8,128)(2,1)S(1)}, u32[]{:S(2)}, u32[]{:S(2)}) %collective-permute-start.12) | collective-permute-done | bytes 331808 | tf_op jit(solution)/shard_map/ppermute | solution.py:264
  58.5 3.4 collective-permute-start.6
  62.0 2.6 broadcast_select_fusion.8
  66.9 6.5 %collective-permute-done.6 = bf16[640,384]{1,0:T(8,128)(2,1)} collective-permute-done((bf16[640,384]{1,0:T(8,128)(2,1)}, bf16[640,384]{1,0:T(8,128)(2,1)}, u32[]{:S(2)}, u32[]{:S(2)}) %collective-permute-start.6) | collective-permute-done | bytes 491552 | tf_op jit(solution)/shard_map/ppermute | solution.py:264
  98.8 2.8 broadcast.173.clone
  101.6 2.5 bitcast_dynamic-update-slice_fusion.8
  108.7 6.9 %collective-permute-done.14 = bf16[1728,384]{1,0:T(8,128)(2,1)} collective-permute-done((bf16[1728,384]{1,0:T(8,128)(2,1)}, bf16[1728,384]{1,0:T(8,128)(2,1)}, u32[]{:S(2)}, u32[]{:S(2)}) %collective-permute-start.14) | collective-permute-done | bytes 1327136 | tf_op jit(solution)/shard_map/ppermute | solution.py:264
  121.7 2.5 bitcast_dynamic-update-slice_fusion.7
  124.2 2.5 bitcast_dynamic-update-slice_fusion.6
  131.8 4.3 fusion.49
  137.2 19.9 %attn_fwd.1 = (bf16[2048,384]{1,0:T(8,128)(2,1)S(1)}, f32[8,2048]{1,0:T(8,128)S(1)}) custom-call(s32[8]{0:T(128)S(1)} %and_select_fusion.lo_ref, s32[8,256]{1,0:T(8,128)S(1)} %reshape.432.start_ref, bf16[2048,384]{1,0:T(8,128)(2,1)S(1)} %get-tuple-element.229.q_ref, bf16[2048,384]{1,0:T(8,128)(2,1)S(1)} %get-tuple-element.228.k_ref, ...), custom_call_target="tpu_custom_call" | custom-call | flops 20000000000 | bytes 6000000 | tf_op jit(solution)/shard_map/attn_fwd/pallas_call | solution.py:104
  157.3 2.9 broadcast.173.clone.1
  160.2 2.6 bitcast_dynamic-update-slice_fusion.4
  168.3 2.6 bitcast_dynamic-update-slice_fusion.3
  170.9 2.5 bitcast_dynamic-update-slice_fusion.2
  174.6 9.1 %broadcast_select_fusion.1 = (bf16[4,1728,384]{2,1,0:T(8,128)(2,1)}, bf16[4,1728,384]{2,1,0:T(8,128)(2,1)}) fusion(bf16[4,1728,384]{2,1,0:T(8,128)(2,1)} %bitcast_dynamic-update-slice_fusion.5, bf16[4,1728,384]{2,1,0:T(8,128)(2,1)} %bitcast_dynamic-update-slice_fusion.1, pred[]{:T(512)S(6)} %eq.28), kind=kLoop, calls=%fused_computation.14 | loop fusion | flops 5308416 | bytes 21233664 | tf_op jit(solution)/shard_map/jit(_where)/select_n | solution.py:462
  183.7 2.2 fusion.98
  185.9 2.3 slice.712
  195.2 5.2 fusion.96
  200.4 10.4 %fusion.94 = f32[3072,768]{1,0:T(8,128)} fusion(bf16[512,768]{1,0:T(8,128)(2,1)S(1)} %copy-done.32, bf16[512,768]{1,0:T(8,128)(2,1)S(1)} %copy-done.31, f32[1024,3072]{1,0:T(8,128)S(1)} %fusion.96, f32[3072]{0:T(1024)S(1)} %copy-done.73), kind=kOutput, calls=%fused_computation.393 | convolution fusion | flops 4866441216 | bytes 23605248 | tf_op jit(solution)/shard_map/dot_general | solution.py:24
  210.9 14.4 %convert_reduce_fusion = (f32[3072]{0:T(1024)S(1)}, bf16[1024,3072]{1,0:T(8,128)(2,1)S(1)}) fusion(f32[1024,3072]{1,0:T(8,128)} %copy-done.79, f32[3072]{0:T(1024)S(1)} %copy-done.73, bf16[3072,384]{1,0:T(8,128)(2,1)S(1)} %bitcast.528, bf16[3072,384]{1,0:T(8,128)(2,1)} %bitcast.530, bf16[512,768]{1,0:T(8,128)(2,1)S(1)} %copy-done.32, ...), kind=kOutput, calls=%fused_computation.10 | convolution fusion | flops 4913624064 | bytes 25190400 | tf_op jit(solution)/shard_map/dot_general | solution.py:24
  225.3 8.2 %multiply_reduce_fusion = (f32[768]{0:T(1024)S(1)}, f32[1024]{0:T(1024)S(1)}, f32[1024]{0:T(1024)S(1)}, f32[768]{0:T(1024)S(1)}, f32[1024,768]{1,0:T(8,128)S(1)}) fusion(f32[1024,768]{1,0:T(8,128)S(1)} %get-tuple-element.346, f32[1024]{0:T(1024)S(1)} %add_rsqrt_fusion, f32[1024]{0:T(1024)S(1)} %broadcast_multiply_fusion.4, f32[768]{0:T(1024)S(1)} %mul.163, ...), kind=kOutput, calls=%fused_computation.52 | convolution fusion | flops 4838912000 | bytes 17327104 | tf_op jit(solution)/shard_map/dot_general | solution.py:24
  233.5 2.4 convert_reduce_fusion.3
  236.0 2.6 convolution_convert_fusion
  238.5 2.8 fusion.44
  241.4 8.4 %fusion.95 = f32[768,3072]{1,0:T(8,128)} fusion(bf16[1024,3072]{1,0:T(8,128)(2,1)S(1)} %get-tuple-element.349, f32[1024,768]{1,0:T(8,128)S(1)} %get-tuple-element.346, f32[768]{0:T(1024)S(1)} %add.362, f32[768]{0:T(1024)S(1)} %mul.163, f32[1024]{0:T(1024)S(1)} %add_rsqrt_fusion, f32[1024]{0:T(1024)S(1)} %broadcast_multiply_fusion.4), kind=kOutput, calls=%fused_computation.394 | convolution fusion | flops 4835770368 | bytes 18888704 | tf_op jit(solution)/shard_map/dot_general | solution.py:24
  249.8 12.4 %reshape.468 = f32[4,768,2,384]{3,2,1,0:T(2,128)} reshape(f32[3072,768]{1,0:T(8,128)} %fusion.94) | data formatting | bytes 18874368 | tf_op jit(solution)/shard_map/reshape | solution.py:542
  262.2 8.8 %constant_dynamic-slice_fusion.5 = f32[4,768,1,384]{3,2,1,0:T(1,128)} fusion(f32[4,768,2,384]{3,2,1,0:T(2,128)} %reshape.468, s32[]{:T(128)S(6)} %select_n.423), kind=kLoop, calls=%fused_computation.334 | loop fusion | bytes 9437188 | tf_op jit(solution)/shard_map/jit(dynamic_index_in_dim)/dynamic_slice | solution.py:239
  271.0 5.2 constant_dynamic-slice_fusion.2
  276.2 3.9 reshape.469
  280.1 4.1 constant_dynamic-slice_fusion.4
  284.2 2.1 constant_dynamic-slice_fusion.1
  286.2 12.6 %reshape.470 = f32[4,192,2,4,384]{4,3,2,1,0:T(4,128)} reshape(f32[768,3072]{1,0:T(8,128)} %fusion.95) | data formatting | bytes 18874368 | tf_op jit(solution)/shard_map/reshape | solution.py:544
  298.8 5.3 constant_dynamic-slice_fusion.3
  304.1 4.8 constant_dynamic-slice_fusion
  308.9 10.8 %add_convert_fusion = bf16[1024,768]{1,0:T(8,128)(2,1)S(1)} fusion(f32[1024,768]{1,0:T(8,128)S(1)} %get-tuple-element.346, f32[768]{0:T(1024)S(1)} %copy-done.76, bf16[3072,384]{1,0:T(8,128)(2,1)S(1)} %bitcast.529, bf16[3072,384]{1,0:T(8,128)(2,1)S(1)} %bitcast.531, f32[1024,3072]{1,0:T(8,128)} %copy-done.79, f32[3072]{0:T(1024)S(1)} %copy-done.73), kind=kOutput, calls=%fused_computation.58 | convolution fusion | flops 4875091968 | bytes 22035456 | tf_op jit(solution)/shard_map/dot_general | solution.py:24
  320.7 7.4 %collective-permute-start.22 = (bf16[512,768]{1,0:T(8,128)(2,1)}, bf16[512,768]{1,0:T(8,128)(2,1)}, u32[]{:S(2)}, u32[]{:S(2)}) collective-permute-start(bf16[512,768]{1,0:T(8,128)(2,1)} %get-tuple-element.278), channel_id=1, source_target_pairs={{0,0},{1,16},{2,2},{3,18},{4,4},{5,20},{6,6},{7,22},{8,8},{9,24},{... | collective-permute-start | bytes 2359304 | tf_op jit(solution)/shard_map/ppermute | solution.py:264
  330.1 2.8 bitcast_dynamic-update-slice_fusion
  332.9 2.9 copy.581
  344.9 2.1 fusion.46
  347.2 3.0 copy-done.19
  351.7 40.4 %attn_bwd.1 = (bf16[2048,384]{1,0:T(8,128)(2,1)S(1)}, bf16[2048,384]{1,0:T(8,128)(2,1)S(1)}, bf16[2048,384]{1,0:T(8,128)(2,1)S(1)}) custom-call(s32[8]{0:T(128)S(1)} %copy-done.11, s32[8,256]{1,0:T(8,128)S(1)} %copy-done.9, bf16[2048,384]{1,0:T(8,128)(2,1)S(1)} %copy-done.5, bf16[2048,384]{1,0:T(8,128)(2,1)S(1)} %copy-done.3, ...), custom_call_target="tpu_custom_call" | custom-call | flops 44000002048 | bytes 12000000 | tf_op jit(solution)/shard_map/attn_bwd/pallas_call | solution.py:215
  393.7 4.3 fusion.48
  398.1 4.5 fusion.110
  405.7 4.9 collective-permute-done.30
  416.9 6.2 %collective-permute-done.33 = bf16[576,384]{1,0:T(8,128)(2,1)S(1)} collective-permute-done((bf16[576,384]{1,0:T(8,128)(2,1)S(1)}, bf16[576,384]{1,0:T(8,128)(2,1)S(1)}, u32[]{:S(2)}, u32[]{:S(2)}) %collective-permute-start.33) | collective-permute-done | bytes 442400 | tf_op jit(solution)/shard_map/ppermute | solution.py:264
  425.2 5.6 %collective-permute-done.34 = bf16[2,2,72,384]{3,2,1,0:T(8,128)(2,1)} collective-permute-done((bf16[2,2,72,384]{3,2,1,0:T(8,128)(2,1)S(1)}, bf16[2,2,72,384]{3,2,1,0:T(8,128)(2,1)}, u32[]{:S(2)}, u32[]{:S(2)}) %collective-permute-start.34) | collective-permute-done | bytes 221216 | tf_op jit(solution)/shard_map/ppermute | solution.py:264
  432.9 6.2 %collective-permute-done.35 = bf16[1,2,72,384]{3,2,1,0:T(8,128)(2,1)S(1)} collective-permute-done((bf16[1,2,72,384]{3,2,1,0:T(8,128)(2,1)S(1)}, bf16[1,2,72,384]{3,2,1,0:T(8,128)(2,1)S(1)}, u32[]{:S(2)}, u32[]{:S(2)}) %collective-permute-start.35) | collective-permute-done | bytes 110624 | tf_op jit(solution)/shard_map/ppermute | solution.py:264
  441.7 5.7 %fusion.23 = (f32[768]{0:T(1024)S(1)}, f32[1024]{0:T(1024)S(1)}, f32[1024]{0:T(1024)S(1)}, f32[768]{0:T(1024)S(1)}, f32[1024,768]{1,0:T(8,128)}) fusion(f32[1024]{0:T(1024)S(1)} %copy-done.66, f32[1024]{0:T(1024)S(1)} %copy-done.61, bf16[512,768]{1,0:T(8,128)(2,1)S(1)} %copy-done.15, bf16[512,768]{1,0:T(8,128)(2,1)S(1)} %copy-done.18, ...), kind=kLoop, calls=%fused_computation.43 | loop fusion | flops 11792896 | bytes 9462788 | tf_op jit(solution)/shard_map/reduce_sum | solution.py:589
  449.1 10.4 %convert_add_fusion = f32[4,1728,384]{2,1,0:T(8,128)} fusion(f32[4,1728,384]{2,1,0:T(8,128)} %copy-done.19, bf16[4,1728,384]{2,1,0:T(8,128)(2,1)} %collective-permute-done.42), kind=kLoop, calls=%fused_computation.12 | loop fusion | flops 5308416 | bytes 26542080 | tf_op jit(solution)/shard_map/add | solution.py:553
  466.2 12.5 %collective-permute-done.43 = bf16[864,384]{1,0:T(8,128)(2,1)S(1)} collective-permute-done((bf16[864,384]{1,0:T(8,128)(2,1)S(1)}, bf16[864,384]{1,0:T(8,128)(2,1)S(1)}, u32[]{:S(2)}, u32[]{:S(2)}) %collective-permute-start.43) | collective-permute-done | bytes 663584 | tf_op jit(solution)/shard_map/ppermute | solution.py:264
  479.7 2.0 fusion.39
  485.5 3.8 fusion.22
  489.4 23.9 %collective-permute-done.46 = bf16[1728,384]{1,0:T(8,128)(2,1)} collective-permute-done((bf16[1728,384]{1,0:T(8,128)(2,1)}, bf16[1728,384]{1,0:T(8,128)(2,1)}, u32[]{:S(2)}, u32[]{:S(2)}) %collective-permute-start.46) | collective-permute-done | bytes 1327136 | tf_op jit(solution)/shard_map/ppermute | solution.py:264
  514.9 2.9 fusion.28
  518.5 2.1 collective-permute-start.41
  522.0 8.9 %collective-permute-done.41 = f32[1,288]{1,0:T(1,128)S(1)} collective-permute-done((f32[1,288]{1,0:T(1,128)S(1)}, f32[1,288]{1,0:T(1,128)S(1)}, u32[]{:S(2)}, u32[]{:S(2)}) %collective-permute-start.41) | collective-permute-done | bytes 1184 | tf_op jit(solution)/shard_map/ppermute | solution.py:264
  530.9 2.2 collective-permute-done.47
  535.7 12.3 %collective-permute-done.48 = bf16[1,2,216,384]{3,2,1,0:T(8,128)(2,1)S(1)} collective-permute-done((bf16[1,2,216,384]{3,2,1,0:T(8,128)(2,1)S(1)}, bf16[1,2,216,384]{3,2,1,0:T(8,128)(2,1)S(1)}, u32[]{:S(2)}, u32[]{:S(2)}) %collective-permute-start.48) | collective-permute-done | bytes 331808 | tf_op jit(solution)/shard_map/ppermute | solution.py:264
  (481 shorter events, 134.1 us)
Async XLA Ops:
  8.8 10.8 %collective-permute-start.2 = (bf16[80,384]{1,0:T(8,128)(2,1)}, bf16[80,384]{1,0:T(8,128)(2,1)}, u32[]{:S(2)}, u32[]{:S(2)}) collective-permute-start(bf16[80,384]{1,0:T(8,128)(2,1)} %fusion.80), channel_id=1, source_target_pairs={{0,1},{1,0},{2,3},{3,2},{4,5},{5,4},{6,7},{7,6},{8,9},{9,8},{10,11... | collective-permute-start | bytes 184328 | tf_op jit(solution)/shard_map/ppermute | solution.py:264
  13.4 19.4 %collective-permute-start.11 = (bf16[216,384]{1,0:T(8,128)(2,1)}, bf16[216,384]{1,0:T(8,128)(2,1)}, u32[]{:S(2)}, u32[]{:S(2)}) collective-permute-start(bf16[216,384]{1,0:T(8,128)(2,1)} %fusion.72), channel_id=1, source_target_pairs={{0,1},{1,0},{2,3},{3,2},{4,5},{5,4},{6,7},{7,6},{8,9},{9,8},{10,11... | collective-permute-start | bytes 497672 | tf_op jit(solution)/shard_map/ppermute | solution.py:264
  14.9 49.6 %collective-permute-start = (bf16[520,768]{1,0:T(8,128)(2,1)}, bf16[520,768]{1,0:T(8,128)(2,1)S(1)}, u32[]{:S(2)}, u32[]{:S(2)}) collective-permute-start(bf16[520,768]{1,0:T(8,128)(2,1)} %get-tuple-element.261), channel_id=1, source_target_pairs={{0,0},{1,16},{2,2},{3,18},{4,4},{5,20},{6,6},{7,22},{8,8},{9,24},{... | collective-permute-start | bytes 2396168 | tf_op jit(solution)/shard_map/ppermute | solution.py:264
  16.7 47.8 %collective-permute-start.1 = (bf16[520,768]{1,0:T(8,128)(2,1)}, bf16[520,768]{1,0:T(8,128)(2,1)}, u32[]{:S(2)}, u32[]{:S(2)}) collective-permute-start(bf16[520,768]{1,0:T(8,128)(2,1)} %get-tuple-element.262), channel_id=1, source_target_pairs={{0,8},{1,24},{2,10},{3,26},{4,12},{5,28},{6,14},{7,30},{8,0},{9,16... | collective-permute-start | bytes 2396168 | tf_op jit(solution)/shard_map/ppermute | solution.py:264
  20.5 11.6 %collective-permute-start.3 = (bf16[1,2,80,384]{3,2,1,0:T(8,128)(2,1)S(1)}, bf16[1,2,80,384]{3,2,1,0:T(8,128)(2,1)S(1)}, u32[]{:S(2)}, u32[]{:S(2)}) collective-permute-start(bf16[1,2,80,384]{3,2,1,0:T(8,128)(2,1)S(1)} %maximum_bitcast_fusion.4), channel_id=1, source_target_pairs={{0,4},{1,5},{2,6},{3,7},{4,0},{5,1},{6,2},{7,3},{8,12},{9,13},{10,... | collective-permute-start | bytes 368648 | tf_op jit(solution)/shard_map/ppermute | solution.py:264
  24.5 34.0 %collective-permute-start.24 = (bf16[512,768]{1,0:T(8,128)(2,1)}, bf16[512,768]{1,0:T(8,128)(2,1)}, u32[]{:S(2)}, u32[]{:S(2)}) collective-permute-start(bf16[512,768]{1,0:T(8,128)(2,1)} %get-tuple-element.274), channel_id=1, source_target_pairs={{0,0},{1,16},{2,2},{3,18},{4,4},{5,20},{6,6},{7,22},{8,8},{9,24},{... | collective-permute-start | bytes 2359304 | tf_op jit(solution)/shard_map/ppermute | solution.py:264
  32.1 29.8 %collective-permute-start.25 = (bf16[512,768]{1,0:T(8,128)(2,1)}, bf16[512,768]{1,0:T(8,128)(2,1)S(1)}, u32[]{:S(2)}, u32[]{:S(2)}) collective-permute-start(bf16[512,768]{1,0:T(8,128)(2,1)} %get-tuple-element.275), channel_id=1, source_target_pairs={{0,8},{1,24},{2,10},{3,26},{4,12},{5,28},{6,14},{7,30},{8,0},{9,16... | collective-permute-start | bytes 2359304 | tf_op jit(solution)/shard_map/ppermute | solution.py:264
  32.8 6.3 %collective-permute-start.4 = (bf16[2,2,80,384]{3,2,1,0:T(8,128)(2,1)S(1)}, bf16[2,2,80,384]{3,2,1,0:T(8,128)(2,1)S(1)}, u32[]{:S(2)}, u32[]{:S(2)}) collective-permute-start(bf16[2,2,80,384]{3,2,1,0:T(8,128)(2,1)S(1)} %maximum_bitcast_fusion.3), channel_id=1, source_target_pairs={{0,2},{1,3},{2,0},{3,1},{4,6},{5,7},{6,4},{7,5},{8,10},{9,11},{10,... | collective-permute-start | bytes 737288 | tf_op jit(solution)/shard_map/ppermute | solution.py:264
  39.1 16.4 %collective-permute-start.12 = (bf16[1,2,216,384]{3,2,1,0:T(8,128)(2,1)S(1)}, bf16[1,2,216,384]{3,2,1,0:T(8,128)(2,1)S(1)}, u32[]{:S(2)}, u32[]{:S(2)}) collective-permute-start(bf16[1,2,216,384]{3,2,1,0:T(8,128)(2,1)S(1)} %maximum_bitcast_fusion.2), channel_id=1, source_target_pairs={{0,4},{1,5},{2,6},{3,7},{4,0},{5,1},{6,2},{7,3},{8,12},{9,13},{10,... | collective-permute-start | bytes 995336 | tf_op jit(solution)/shard_map/ppermute | solution.py:264
  55.5 19.2 %collective-permute-start.5 = (bf16[640,384]{1,0:T(8,128)(2,1)}, bf16[640,384]{1,0:T(8,128)(2,1)}, u32[]{:S(2)}, u32[]{:S(2)}) collective-permute-start(bf16[640,384]{1,0:T(8,128)(2,1)} %bitcast.17), channel_id=1, source_target_pairs={{0,8},{1,9},{2,10},{3,11},{4,12},{5,13},{6,14},{7,15},{8,0},{9,1},... | collective-permute-start | bytes 1474568 | tf_op jit(solution)/shard_map/ppermute | solution.py:264
  58.5 14.9 %collective-permute-start.6 = (bf16[640,384]{1,0:T(8,128)(2,1)}, bf16[640,384]{1,0:T(8,128)(2,1)}, u32[]{:S(2)}, u32[]{:S(2)}) collective-permute-start(bf16[640,384]{1,0:T(8,128)(2,1)} %bitcast.17), channel_id=1, source_target_pairs={{0,16},{1,17},{2,18},{3,19},{4,20},{5,21},{6,22},{7,23},{8,24},{9,... | collective-permute-start | bytes 1474568 | tf_op jit(solution)/shard_map/ppermute | solution.py:264
  62.0 17.8 %collective-permute-start.13 = (bf16[2,2,216,384]{3,2,1,0:T(8,128)(2,1)}, bf16[2,2,216,384]{3,2,1,0:T(8,128)(2,1)}, u32[]{:S(2)}, u32[]{:S(2)}) collective-permute-start(bf16[2,2,216,384]{3,2,1,0:T(8,128)(2,1)} %maximum_bitcast_fusion), channel_id=1, source_target_pairs={{0,2},{1,3},{2,0},{3,1},{4,6},{5,7},{6,4},{7,5},{8,10},{9,11},{10,... | collective-permute-start | bytes 1990664 | tf_op jit(solution)/shard_map/ppermute | solution.py:264
  65.8 28.6 %copy-start.13 = (bf16[512,768]{1,0:T(8,128)(2,1)}, bf16[512,768]{1,0:T(8,128)(2,1)S(1)}, u32[]{:S(2)}) copy-start(bf16[512,768]{1,0:T(8,128)(2,1)S(1)} %slice.654) | copy-start | bytes 2359300
  65.9 28.5 %copy-start.16 = (bf16[512,768]{1,0:T(8,128)(2,1)}, bf16[512,768]{1,0:T(8,128)(2,1)S(1)}, u32[]{:S(2)}) copy-start(bf16[512,768]{1,0:T(8,128)(2,1)S(1)} %slice.653) | copy-start | bytes 2359300
  66.2 28.2 %copy-start.60 = (f32[1024]{0:T(1024)}, f32[1024]{0:T(1024)S(1)}, u32[]{:S(2)}) copy-start(f32[1024]{0:T(1024)S(1)} %broadcast_multiply_fusion.5) | copy-start | bytes 12292
  66.9 27.6 %copy-start.65 = (f32[1024]{0:T(1024)}, f32[1024]{0:T(1024)S(1)}, u32[]{:S(2)}) copy-start(f32[1024]{0:T(1024)S(1)} %add_rsqrt_fusion.1) | copy-start | bytes 12292
  74.4 13.3 %collective-permute-start.8 = (bf16[320,384]{1,0:T(8,128)(2,1)S(1)}, bf16[320,384]{1,0:T(8,128)(2,1)S(1)}, u32[]{:S(2)}, u32[]{:S(2)}) collective-permute-start(bf16[320,384]{1,0:T(8,128)(2,1)S(1)} %slice.662), channel_id=1, source_target_pairs={{0,8},{1,9},{2,10},{3,11},{4,12},{5,13},{6,14},{7,15},{8,0},{9,1},... | collective-permute-start | bytes 737288 | tf_op jit(solution)/shard_map/ppermute | solution.py:264
  75.7 12.0 %collective-permute-start.7 = (bf16[320,384]{1,0:T(8,128)(2,1)S(1)}, bf16[320,384]{1,0:T(8,128)(2,1)S(1)}, u32[]{:S(2)}, u32[]{:S(2)}) collective-permute-start(bf16[320,384]{1,0:T(8,128)(2,1)S(1)} %slice.661), channel_id=1, source_target_pairs={{0,16},{1,17},{2,18},{3,19},{4,20},{5,21},{6,22},{7,23},{8,24},{9,... | collective-permute-start | bytes 737288 | tf_op jit(solution)/shard_map/ppermute | solution.py:264
  85.6 30.0 %collective-permute-start.14 = (bf16[1728,384]{1,0:T(8,128)(2,1)}, bf16[1728,384]{1,0:T(8,128)(2,1)}, u32[]{:S(2)}, u32[]{:S(2)}) collective-permute-start(bf16[1728,384]{1,0:T(8,128)(2,1)} %constant_dynamic-update-slice_fusion.12), channel_id=1, source_target_pairs={{0,8},{1,9},{2,10},{3,11},{4,12},{5,13},{6,14},{7,15},{8,0},{9,1},... | collective-permute-start | bytes 3981320 | tf_op jit(solution)/shard_map/ppermute | solution.py:264
  87.4 30.9 %collective-permute-start.15 = (bf16[1728,384]{1,0:T(8,128)(2,1)}, bf16[1728,384]{1,0:T(8,128)(2,1)}, u32[]{:S(2)}, u32[]{:S(2)}) collective-permute-start(bf16[1728,384]{1,0:T(8,128)(2,1)} %constant_dynamic-update-slice_fusion.12), channel_id=1, source_target_pairs={{0,16},{1,17},{2,18},{3,19},{4,20},{5,21},{6,22},{7,23},{8,24},{9,... | collective-permute-start | bytes 3981320 | tf_op jit(solution)/shard_map/ppermute | solution.py:264
  87.7 69.6 %collective-permute-start.18 = (bf16[1728,384]{1,0:T(8,128)(2,1)}, bf16[1728,384]{1,0:T(8,128)(2,1)}, u32[]{:S(2)}, u32[]{:S(2)}) collective-permute-start(bf16[1728,384]{1,0:T(8,128)(2,1)} %constant_dynamic-update-slice_fusion.12), channel_id=1, source_target_pairs={{0,1},{1,0},{2,3},{3,2},{4,5},{5,4},{6,7},{7,6},{8,9},{9,8},{10,11... | collective-permute-start | bytes 3981320 | tf_op jit(solution)/shard_map/ppermute | solution.py:264
  98.3 28.5 %collective-permute-start.9 = (bf16[1040,768]{1,0:T(8,128)(2,1)}, bf16[1040,768]{1,0:T(8,128)(2,1)}, u32[]{:S(2)}, u32[]{:S(2)}) collective-permute-start(bf16[1040,768]{1,0:T(8,128)(2,1)} %fusion.32), channel_id=1, source_target_pairs={{0,1},{1,0},{2,3},{3,2},{4,5},{5,4},{6,7},{7,6},{8,9},{9,8},{10,11... | collective-permute-start | bytes 4792328 | tf_op jit(solution)/shard_map/ppermute | solution.py:264
  117.6 45.2 %collective-permute-start.16 = (bf16[864,384]{1,0:T(8,128)(2,1)}, bf16[864,384]{1,0:T(8,128)(2,1)}, u32[]{:S(2)}, u32[]{:S(2)}) collective-permute-start(bf16[864,384]{1,0:T(8,128)(2,1)} %slice.695), channel_id=1, source_target_pairs={{0,16},{1,17},{2,18},{3,19},{4,20},{5,21},{6,22},{7,23},{8,24},{9,... | collective-permute-start | bytes 1990664 | tf_op jit(solution)/shard_map/ppermute | solution.py:264
  120.2 43.7 %collective-permute-start.17 = (bf16[864,384]{1,0:T(8,128)(2,1)}, bf16[864,384]{1,0:T(8,128)(2,1)}, u32[]{:S(2)}, u32[]{:S(2)}) collective-permute-start(bf16[864,384]{1,0:T(8,128)(2,1)} %slice.696), channel_id=1, source_target_pairs={{0,8},{1,9},{2,10},{3,11},{4,12},{5,13},{6,14},{7,15},{8,0},{9,1},... | collective-permute-start | bytes 1990664 | tf_op jit(solution)/shard_map/ppermute | solution.py:264
  121.7 46.6 %collective-permute-start.19 = (bf16[1728,384]{1,0:T(8,128)(2,1)}, bf16[1728,384]{1,0:T(8,128)(2,1)}, u32[]{:S(2)}, u32[]{:S(2)}) collective-permute-start(bf16[1728,384]{1,0:T(8,128)(2,1)} %collective-permute-done.14), channel_id=1, source_target_pairs={{0,1},{1,0},{2,3},{3,2},{4,5},{5,4},{6,7},{7,6},{8,9},{9,8},{10,11... | collective-permute-start | bytes 3981320 | tf_op jit(solution)/shard_map/ppermute | solution.py:264
  126.7 44.1 %collective-permute-start.20 = (bf16[1728,384]{1,0:T(8,128)(2,1)}, bf16[1728,384]{1,0:T(8,128)(2,1)}, u32[]{:S(2)}, u32[]{:S(2)}) collective-permute-start(bf16[1728,384]{1,0:T(8,128)(2,1)} %collective-permute-done.15), channel_id=1, source_target_pairs={{0,1},{1,0},{2,3},{3,2},{4,5},{5,4},{6,7},{7,6},{8,9},{9,8},{10,11... | collective-permute-start | bytes 3981320 | tf_op jit(solution)/shard_map/ppermute | solution.py:264
  136.9 20.2 %copy-start.2 = (bf16[2048,384]{1,0:T(8,128)(2,1)}, bf16[2048,384]{1,0:T(8,128)(2,1)S(1)}, u32[]{:S(2)}) copy-start(bf16[2048,384]{1,0:T(8,128)(2,1)S(1)} %get-tuple-element.228.k_ref) | copy-start | bytes 4718596
  136.9 20.2 %copy-start.4 = (bf16[2048,384]{1,0:T(8,128)(2,1)}, bf16[2048,384]{1,0:T(8,128)(2,1)S(1)}, u32[]{:S(2)}) copy-start(bf16[2048,384]{1,0:T(8,128)(2,1)S(1)} %get-tuple-element.229.q_ref) | copy-start | bytes 4718596
  137.2 19.9 %copy-start.6 = (bf16[2048,384]{1,0:T(8,128)(2,1)}, bf16[2048,384]{1,0:T(8,128)(2,1)S(1)}, u32[]{:S(2)}) copy-start(bf16[2048,384]{1,0:T(8,128)(2,1)S(1)} %fusion.25.v_ref) | copy-start | bytes 4718596
  157.3 9.7 %collective-permute-start.10 = (bf16[1024,384]{1,0:T(8,128)(2,1)S(1)}, bf16[1024,384]{1,0:T(8,128)(2,1)S(1)}, u32[]{:S(2)}, u32[]{:S(2)}) collective-permute-start(bf16[1024,384]{1,0:T(8,128)(2,1)S(1)} %dynamic-slice_bitcast_fusion.2), channel_id=1, source_target_pairs={{0,1},{1,0},{2,3},{3,2},{4,5},{5,4},{6,7},{7,6},{8,9},{9,8},{10,11... | collective-permute-start | bytes 2359304 | tf_op jit(solution)/shard_map/ppermute | solution.py:264
  165.2 8.2 %collective-permute-start.21 = (bf16[1728,384]{1,0:T(8,128)(2,1)S(1)}, bf16[1728,384]{1,0:T(8,128)(2,1)S(1)}, u32[]{:S(2)}, u32[]{:S(2)}) collective-permute-start(bf16[1728,384]{1,0:T(8,128)(2,1)S(1)} %constant_dynamic-update-slice_fusion.18), channel_id=1, source_target_pairs={{0,1},{1,0},{2,3},{3,2},{4,5},{5,4},{6,7},{7,6},{8,9},{9,8},{10,11... | collective-permute-start | bytes 3981320 | tf_op jit(solution)/shard_map/ppermute | solution.py:264
  188.3 22.6 %copy-start.38 = (bf16[4,768,384]{2,1,0:T(8,128)(2,1)}, bf16[4,768,384]{2,1,0:T(8,128)(2,1)S(1)}, u32[]{:S(2)}) copy-start(bf16[4,768,384]{2,1,0:T(8,128)(2,1)S(1)} %slice.712) | copy-start | bytes 7077892
  320.7 94.7 %collective-permute-start.22 = (bf16[512,768]{1,0:T(8,128)(2,1)}, bf16[512,768]{1,0:T(8,128)(2,1)}, u32[]{:S(2)}, u32[]{:S(2)}) collective-permute-start(bf16[512,768]{1,0:T(8,128)(2,1)} %get-tuple-element.278), channel_id=1, source_target_pairs={{0,0},{1,16},{2,2},{3,18},{4,4},{5,20},{6,6},{7,22},{8,8},{9,24},{... | collective-permute-start | bytes 2359304 | tf_op jit(solution)/shard_map/ppermute | solution.py:264
  328.2 87.3 %collective-permute-start.23 = (bf16[512,768]{1,0:T(8,128)(2,1)S(1)}, bf16[512,768]{1,0:T(8,128)(2,1)}, u32[]{:S(2)}, u32[]{:S(2)}) collective-permute-start(bf16[512,768]{1,0:T(8,128)(2,1)S(1)} %get-tuple-element.279), channel_id=1, source_target_pairs={{0,8},{1,24},{2,10},{3,26},{4,12},{5,28},{6,14},{7,30},{8,0},{9,16... | collective-permute-start | bytes 2359304 | tf_op jit(solution)/shard_map/ppermute | solution.py:264
  329.2 15.7 %collective-permute-start.26 = (bf16[1024,384]{1,0:T(8,128)(2,1)S(1)}, bf16[1024,384]{1,0:T(8,128)(2,1)}, u32[]{:S(2)}, u32[]{:S(2)}) collective-permute-start(bf16[1024,384]{1,0:T(8,128)(2,1)S(1)} %bitcast.543), channel_id=1, source_target_pairs={{0,1},{1,0},{2,3},{3,2},{4,5},{5,4},{6,7},{7,6},{8,9},{9,8},{10,11... | collective-permute-start | bytes 2359304 | tf_op jit(solution)/shard_map/ppermute | solution.py:264
  343.9 105.2 %collective-permute-start.42 = (bf16[4,1728,384]{2,1,0:T(8,128)(2,1)}, bf16[4,1728,384]{2,1,0:T(8,128)(2,1)}, u32[]{:S(2)}, u32[]{:S(2)}) collective-permute-start(bf16[4,1728,384]{2,1,0:T(8,128)(2,1)} %fusion.55), channel_id=1, source_target_pairs={{0,1},{1,0},{2,3},{3,2},{4,5},{5,4},{6,7},{7,6},{8,9},{9,8},{10,11... | collective-permute-start | bytes 15925256 | tf_op jit(solution)/shard_map/ppermute | solution.py:264
  398.1 16.0 %copy-start.28 = (f32[2048,768]{1,0:T(8,128)}, f32[2048,768]{1,0:T(8,128)S(1)}, u32[]{:S(2)}) copy-start(f32[2048,768]{1,0:T(8,128)S(1)} %fusion.48) | copy-start | bytes 18874372
  403.2 7.4 %collective-permute-start.30 = (bf16[288,384]{1,0:T(8,128)(2,1)S(1)}, bf16[288,384]{1,0:T(8,128)(2,1)S(1)}, u32[]{:S(2)}, u32[]{:S(2)}) collective-permute-start(bf16[288,384]{1,0:T(8,128)(2,1)S(1)} %get-tuple-element.297), channel_id=1, source_target_pairs={{0,16},{1,17},{2,18},{3,19},{4,20},{5,21},{6,22},{7,23},{8,24},{9,... | collective-permute-start | bytes 663560 | tf_op jit(solution)/shard_map/ppermute | solution.py:264
  403.9 7.5 %collective-permute-start.32 = (bf16[288,384]{1,0:T(8,128)(2,1)S(1)}, bf16[288,384]{1,0:T(8,128)(2,1)S(1)}, u32[]{:S(2)}, u32[]{:S(2)}) collective-permute-start(bf16[288,384]{1,0:T(8,128)(2,1)S(1)} %get-tuple-element.298), channel_id=1, source_target_pairs={{0,8},{1,9},{2,10},{3,11},{4,12},{5,13},{6,14},{7,15},{8,0},{9,1},... | collective-permute-start | bytes 663560 | tf_op jit(solution)/shard_map/ppermute | solution.py:264
  411.6 11.5 %collective-permute-start.33 = (bf16[576,384]{1,0:T(8,128)(2,1)S(1)}, bf16[576,384]{1,0:T(8,128)(2,1)S(1)}, u32[]{:S(2)}, u32[]{:S(2)}) collective-permute-start(bf16[576,384]{1,0:T(8,128)(2,1)S(1)} %pad_maximum_fusion.26), channel_id=1, source_target_pairs={{0,16},{1,17},{2,18},{3,19},{4,20},{5,21},{6,22},{7,23},{8,24},{9,... | collective-permute-start | bytes 1327112 | tf_op jit(solution)/shard_map/ppermute | solution.py:264
  412.6 11.0 %collective-permute-start.31 = (bf16[576,384]{1,0:T(8,128)(2,1)S(1)}, bf16[576,384]{1,0:T(8,128)(2,1)S(1)}, u32[]{:S(2)}, u32[]{:S(2)}) collective-permute-start(bf16[576,384]{1,0:T(8,128)(2,1)S(1)} %pad_maximum_fusion.25), channel_id=1, source_target_pairs={{0,8},{1,9},{2,10},{3,11},{4,12},{5,13},{6,14},{7,15},{8,0},{9,1},... | collective-permute-start | bytes 1327112 | tf_op jit(solution)/shard_map/ppermute | solution.py:264
  415.4 26.2 %collective-permute-start.27 = (bf16[1024,768]{1,0:T(8,128)(2,1)}, bf16[1024,768]{1,0:T(8,128)(2,1)}, u32[]{:S(2)}, u32[]{:S(2)}) collective-permute-start(bf16[1024,768]{1,0:T(8,128)(2,1)} %fusion.34), channel_id=1, source_target_pairs={{0,1},{1,0},{2,3},{3,2},{4,5},{5,4},{6,7},{7,6},{8,9},{9,8},{10,11... | collective-permute-start | bytes 4718600 | tf_op jit(solution)/shard_map/ppermute | solution.py:264
  424.7 6.1 %collective-permute-start.34 = (bf16[2,2,72,384]{3,2,1,0:T(8,128)(2,1)S(1)}, bf16[2,2,72,384]{3,2,1,0:T(8,128)(2,1)}, u32[]{:S(2)}, u32[]{:S(2)}) collective-permute-start(bf16[2,2,72,384]{3,2,1,0:T(8,128)(2,1)S(1)} %fusion.66), channel_id=1, source_target_pairs={{0,2},{1,3},{2,0},{3,1},{4,6},{5,7},{6,4},{7,5},{8,10},{9,11},{10,... | collective-permute-start | bytes 663560 | tf_op jit(solution)/shard_map/ppermute | solution.py:264
  425.2 16.4 %copy-start.15 = (bf16[512,768]{1,0:T(8,128)(2,1)S(1)}, bf16[512,768]{1,0:T(8,128)(2,1)}, u32[]{:S(2)}) copy-start(bf16[512,768]{1,0:T(8,128)(2,1)} %copy-done.13) | copy-start | bytes 2359300
  425.2 16.4 %copy-start.18 = (bf16[512,768]{1,0:T(8,128)(2,1)S(1)}, bf16[512,768]{1,0:T(8,128)(2,1)}, u32[]{:S(2)}) copy-start(bf16[512,768]{1,0:T(8,128)(2,1)} %copy-done.16) | copy-start | bytes 2359300
  425.2 16.4 %copy-start.61 = (f32[1024]{0:T(1024)S(1)}, f32[1024]{0:T(1024)}, u32[]{:S(2)}) copy-start(f32[1024]{0:T(1024)} %copy-done.60) | copy-start | bytes 12292
  425.2 16.4 %copy-start.64 = (f32[768]{0:T(1024)S(1)}, f32[768]{0:T(1024)}, u32[]{:S(2)}) copy-start(f32[768]{0:T(1024)} %copy-done.63) | copy-start | bytes 9220
  425.2 16.4 %copy-start.66 = (f32[1024]{0:T(1024)S(1)}, f32[1024]{0:T(1024)}, u32[]{:S(2)}) copy-start(f32[1024]{0:T(1024)} %copy-done.65) | copy-start | bytes 12292
  432.8 6.3 %collective-permute-start.35 = (bf16[1,2,72,384]{3,2,1,0:T(8,128)(2,1)S(1)}, bf16[1,2,72,384]{3,2,1,0:T(8,128)(2,1)S(1)}, u32[]{:S(2)}, u32[]{:S(2)}) collective-permute-start(bf16[1,2,72,384]{3,2,1,0:T(8,128)(2,1)S(1)} %dynamic-slice_convert_fusion.9), channel_id=1, source_target_pairs={{0,4},{1,5},{2,6},{3,7},{4,0},{5,1},{6,2},{7,3},{8,12},{9,13},{10,... | collective-permute-start | bytes 331784 | tf_op jit(solution)/shard_map/ppermute | solution.py:264
  440.1 1.4 collective-permute-start.36
  447.6 16.0 %collective-permute-start.37 = (f32[2,8,288]{2,1,0:T(8,128)S(1)}, f32[2,8,288]{2,1,0:T(8,128)S(1)}, u32[]{:S(2)}, u32[]{:S(2)}) collective-permute-start(f32[2,8,288]{2,1,0:T(8,128)S(1)} %dynamic-slice_bitcast_fusion.7), channel_id=1, source_target_pairs={{0,8},{1,9},{2,10},{3,11},{4,12},{5,13},{6,14},{7,15},{8,0},{9,1},... | collective-permute-start | bytes 55304 | tf_op jit(solution)/shard_map/ppermute | solution.py:264
  461.5 17.2 %collective-permute-start.43 = (bf16[864,384]{1,0:T(8,128)(2,1)S(1)}, bf16[864,384]{1,0:T(8,128)(2,1)S(1)}, u32[]{:S(2)}, u32[]{:S(2)}) collective-permute-start(bf16[864,384]{1,0:T(8,128)(2,1)S(1)} %get-tuple-element.280), channel_id=1, source_target_pairs={{0,16},{1,17},{2,18},{3,19},{4,20},{5,21},{6,22},{7,23},{8,24},{9,... | collective-permute-start | bytes 1990664 | tf_op jit(solution)/shard_map/ppermute | solution.py:264
  463.0 16.7 %collective-permute-start.45 = (bf16[864,384]{1,0:T(8,128)(2,1)S(1)}, bf16[864,384]{1,0:T(8,128)(2,1)S(1)}, u32[]{:S(2)}, u32[]{:S(2)}) collective-permute-start(bf16[864,384]{1,0:T(8,128)(2,1)S(1)} %get-tuple-element.281), channel_id=1, source_target_pairs={{0,8},{1,9},{2,10},{3,11},{4,12},{5,13},{6,14},{7,15},{8,0},{9,1},... | collective-permute-start | bytes 1990664 | tf_op jit(solution)/shard_map/ppermute | solution.py:264
  463.6 21.7 %collective-permute-start.38 = (f32[1,8,288]{2,1,0:T(8,128)S(1)}, f32[1,8,288]{2,1,0:T(8,128)S(1)}, u32[]{:S(2)}, u32[]{:S(2)}) collective-permute-start(f32[1,8,288]{2,1,0:T(8,128)S(1)} %constant_dynamic-slice_fusion.12), channel_id=1, source_target_pairs={{0,16},{1,17},{2,18},{3,19},{4,20},{5,21},{6,22},{7,23},{8,24},{9,... | collective-permute-start | bytes 27656 | tf_op jit(solution)/shard_map/ppermute | solution.py:264
  483.0 30.4 %collective-permute-start.46 = (bf16[1728,384]{1,0:T(8,128)(2,1)}, bf16[1728,384]{1,0:T(8,128)(2,1)}, u32[]{:S(2)}, u32[]{:S(2)}) collective-permute-start(bf16[1728,384]{1,0:T(8,128)(2,1)} %pad_maximum_fusion.16), channel_id=1, source_target_pairs={{0,16},{1,17},{2,18},{3,19},{4,20},{5,21},{6,22},{7,23},{8,24},{9,... | collective-permute-start | bytes 3981320 | tf_op jit(solution)/shard_map/ppermute | solution.py:264
  484.8 30.1 %collective-permute-start.44 = (bf16[1728,384]{1,0:T(8,128)(2,1)}, bf16[1728,384]{1,0:T(8,128)(2,1)}, u32[]{:S(2)}, u32[]{:S(2)}) collective-permute-start(bf16[1728,384]{1,0:T(8,128)(2,1)} %pad_maximum_fusion.15), channel_id=1, source_target_pairs={{0,8},{1,9},{2,10},{3,11},{4,12},{5,13},{6,14},{7,15},{8,0},{9,1},... | collective-permute-start | bytes 3981320 | tf_op jit(solution)/shard_map/ppermute | solution.py:264
  485.4 3.8 collective-permute-start.39
  489.4 29.1 %collective-permute-start.40 = (f32[2,288]{1,0:T(2,128)S(1)}, f32[2,288]{1,0:T(2,128)S(1)}, u32[]{:S(2)}, u32[]{:S(2)}) collective-permute-start(f32[2,288]{1,0:T(2,128)S(1)} %bitcast.562), channel_id=1, source_target_pairs={{0,2},{1,3},{2,0},{3,1},{4,6},{5,7},{6,4},{7,5},{8,10},{9,11},{10,... | collective-permute-start | bytes 6920 | tf_op jit(solution)/shard_map/ppermute | solution.py:264
  518.3 14.8 %collective-permute-start.47 = (bf16[2,2,216,384]{3,2,1,0:T(8,128)(2,1)S(1)}, bf16[2,2,216,384]{3,2,1,0:T(8,128)(2,1)S(1)}, u32[]{:S(2)}, u32[]{:S(2)}) collective-permute-start(bf16[2,2,216,384]{3,2,1,0:T(8,128)(2,1)S(1)} %fusion.50), channel_id=1, source_target_pairs={{0,2},{1,3},{2,0},{3,1},{4,6},{5,7},{6,4},{7,5},{8,10},{9,11},{10,... | collective-permute-start | bytes 1990664 | tf_op jit(solution)/shard_map/ppermute | solution.py:264
  518.5 12.4 %collective-permute-start.41 = (f32[1,288]{1,0:T(1,128)S(1)}, f32[1,288]{1,0:T(1,128)S(1)}, u32[]{:S(2)}, u32[]{:S(2)}) collective-permute-start(f32[1,288]{1,0:T(1,128)S(1)} %constant_dynamic-slice_fusion.6), channel_id=1, source_target_pairs={{0,4},{1,5},{2,6},{3,7},{4,0},{5,1},{6,2},{7,3},{8,12},{9,13},{10,... | collective-permute-start | bytes 3464 | tf_op jit(solution)/shard_map/ppermute | solution.py:264
  520.6 27.6 %collective-permute-start.28 = (bf16[512,768]{1,0:T(8,128)(2,1)S(1)}, bf16[512,768]{1,0:T(8,128)(2,1)S(1)}, u32[]{:S(2)}, u32[]{:S(2)}) collective-permute-start(bf16[512,768]{1,0:T(8,128)(2,1)S(1)} %get-tuple-element.266), channel_id=1, source_target_pairs={{0,0},{1,16},{2,2},{3,18},{4,4},{5,20},{6,6},{7,22},{8,8},{9,24},{... | collective-permute-start | bytes 2359304 | tf_op jit(solution)/shard_map/ppermute | solution.py:264
  521.3 26.9 %collective-permute-start.29 = (bf16[512,768]{1,0:T(8,128)(2,1)S(1)}, bf16[512,768]{1,0:T(8,128)(2,1)S(1)}, u32[]{:S(2)}, u32[]{:S(2)}) collective-permute-start(bf16[512,768]{1,0:T(8,128)(2,1)S(1)} %get-tuple-element.267), channel_id=1, source_target_pairs={{0,8},{1,24},{2,10},{3,26},{4,12},{5,28},{6,14},{7,30},{8,0},{9,16... | collective-permute-start | bytes 2359304 | tf_op jit(solution)/shard_map/ppermute | solution.py:264
  533.3 14.7 %collective-permute-start.48 = (bf16[1,2,216,384]{3,2,1,0:T(8,128)(2,1)S(1)}, bf16[1,2,216,384]{3,2,1,0:T(8,128)(2,1)S(1)}, u32[]{:S(2)}, u32[]{:S(2)}) collective-permute-start(bf16[1,2,216,384]{3,2,1,0:T(8,128)(2,1)S(1)} %dynamic-slice_convert_fusion.5), channel_id=1, source_target_pairs={{0,4},{1,5},{2,6},{3,7},{4,0},{5,1},{6,2},{7,3},{8,12},{9,13},{10,... | collective-permute-start | bytes 995336 | tf_op jit(solution)/shard_map/ppermute | solution.py:264
  548.1 1.7 collective-permute-start.49
  (68 other events, 349.4 us)
